TPU v7x, 32 devices: a whole 2x2x4 slice. The times are simulated.
32 devices in a mesh: dp: 16 (over z, x, core), blk: 2 (over y).
Axes of the slice: x: 2, y: 2, z: 4, core: 2. Of those that a mesh axis runs over, the one named last changes fastest.
Arguments:
- hidden_in: bfloat16 [32, 512, 768], P('dp', 'blk'), may hold values from -6 to 6
- page_lengths: int32 [32], P('dp'), may hold values from 40 to 512, as said below
- pad_mask: int32 [32, 512], P('dp', 'blk'), may hold values from 0 to 1, as said below
- query_weight: bfloat16 [768, 768], P(('dp', 'blk')), may hold values from -0.21875 to 0.21875
- query_bias: bfloat16 [768], P(('dp', 'blk')), may hold values from -1.1953125 to 1.1953125
- key_weight: bfloat16 [768, 768], P(('dp', 'blk')), may hold values from -0.21875 to 0.21875
- value_weight: bfloat16 [768, 768], P(('dp', 'blk')), may hold values from -0.21875 to 0.21875
- value_bias: bfloat16 [768], P(('dp', 'blk')), may hold values from -3 to 3
- output_weight: bfloat16 [768, 768], P(('dp', 'blk')), may hold values from -1.25 to 1.25
- output_bias: bfloat16 [768], P(('dp', 'blk')), may hold values from -3 to 3
- first_gain: bfloat16 [768], P(('dp', 'blk')), may hold values from 0.5 to 1.5
- first_shift: bfloat16 [768], P(('dp', 'blk')), may hold values from -3 to 3
- inner_weight: bfloat16 [768, 3072], P(('dp', 'blk')), may hold values from -0.21875 to 0.21875
- inner_bias: bfloat16 [3072], P(('dp', 'blk')), may hold values from -3 to 3
- outer_weight: bfloat16 [3072, 768], P(('dp', 'blk')), may hold values from -0.109375 to 0.109375
- outer_bias: bfloat16 [768], P(('dp', 'blk')), may hold values from -3 to 3
- second_gain: bfloat16 [768], P(('dp', 'blk')), may hold values from 0.5 to 1.5
- second_shift: bfloat16 [768], P(('dp', 'blk')), may hold values from -3 to 3
- out_grad: bfloat16 [32, 512, 768], P('dp', 'blk'), may hold values from -6 to 6
Outputs:
- output: bfloat16 [32, 512, 768], P('dp', 'blk')
- input_grad: bfloat16 [32, 512, 768], P('dp', 'blk')
- query_weight_grad: float32 [768, 768], P(('dp', 'blk'))
- query_bias_grad: float32 [768], P(('dp', 'blk'))
- key_weight_grad: float32 [768, 768], P(('dp', 'blk'))
- value_weight_grad: float32 [768, 768], P(('dp', 'blk'))
- value_bias_grad: float32 [768], P(('dp', 'blk'))
- output_weight_grad: float32 [768, 768], P(('dp', 'blk'))
- output_bias_grad: float32 [768], P(('dp', 'blk'))
- first_gain_grad: float32 [768], P(('dp', 'blk'))
- first_shift_grad: float32 [768], P(('dp', 'blk'))
- inner_weight_grad: float32 [768, 3072], P(('dp', 'blk'))
- inner_bias_grad: float32 [3072], P(('dp', 'blk'))
- outer_weight_grad: float32 [3072, 768], P(('dp', 'blk'))
- outer_bias_grad: float32 [768], P(('dp', 'blk'))
- second_gain_grad: float32 [768], P(('dp', 'blk'))
- second_shift_grad: float32 [768], P(('dp', 'blk'))
Inputs may be any that keep to these rules, and one draw needn't show every extreme that they name: `page_lengths`: among the 2 pages of each index of dp, at least one has exactly 512 real tokens. `pad_mask`: position 0 of every page is 1.
All inputs are finite; a program needn't handle non-finite values.
Results may differ from a plain program's by a relative error of at most 0.014.
Values may be sent and summed in bfloat16 or wider, within the bound.
A program may use at most 192 MiB of HBM per device.

v0:
```python
from functools import partial

import jax
import jax.numpy as jnp
from jax import lax
from jax.experimental import pallas as pl
from jax.experimental.pallas import tpu as pltpu
from jax.sharding import PartitionSpec as P

HEADS = 12
NEG_FILL = -1000000000.0
EPSILON = 1e-05

NZ, NX, NC, NY = 4, 2, 2, 2
GROUP = NZ * NX * NC
CHUNKS = 6
ROWS, COLS = 96, 384
CUT = 64
WIDTH = 768
BF, F32 = jnp.bfloat16, jnp.float32
VMEM_LIMIT = 62 * 2**20


def rem(a, b):
    return lax.rem(a, b)


class Place:
    def __init__(self, stride):
        dp = lax.axis_index("dp")
        self.y = lax.axis_index("blk")
        index = dp // stride
        self.low = dp - index * stride
        self.stride = stride
        self.z = index // (NX * NC)
        self.x = (index // NC) % NX
        self.c = index % NC
        self.ox, self.oy, self.oc = 1 - self.x, 1 - self.y, 1 - self.c

    def dev(self, z, x, c, y):
        return ((z * (NX * NC) + x * NC + c) * self.stride + self.low, y)

    def above(self, k):
        return rem(self.z + k, NZ)

    def below(self, k):
        return rem(self.z + NZ - k, NZ)

    def to_z(self, k):
        return self.dev(self.above(k), self.x, self.c, self.y)

    @property
    def to_x(self):
        return self.dev(self.z, self.ox, self.c, self.y)

    @property
    def to_y(self):
        return self.dev(self.z, self.x, self.c, self.oy)

    @property
    def to_c(self):
        return self.dev(self.z, self.x, self.oc, self.y)

    def greet(self):
        barrier = pltpu.get_barrier_semaphore()
        partners = [self.to_z(k) for k in range(1, NZ)] + [self.to_x, self.to_y, self.to_c]
        for who in partners:
            pl.semaphore_signal(barrier, inc=1, device_id=who, device_id_type=pl.DeviceIdType.MESH)
        pl.semaphore_wait(barrier, len(partners))


def remote(src, dst, sems, index, who):
    send, recv = sems
    return pltpu.make_async_remote_copy(
        src_ref=src,
        dst_ref=dst,
        send_sem=send.at[index],
        recv_sem=recv.at[index],
        device_id=who,
        device_id_type=pl.DeviceIdType.MESH,
    )


def loop(count, body):
    def step(i, carry):
        body(i)
        return carry

    lax.fori_loop(0, count, step, 0)


class Gather:
    def __init__(self, at, blocks, zs, p1, p2, cs):
        self.at, self.g = at, blocks
        self.zs, self.p1, self.p2, self.cs = zs, p1, p2, cs

    def z_copy(self, ch, k, mine=True):
        at = self.at
        z = at.z if mine else at.below(k)
        ref = self.g.at[ch, z, at.x, at.c, at.y]
        return remote(ref, ref, self.zs, (ch, k - 1), at.to_z(k))

    def p1_copies(self, ch, k, mine=True):
        at = self.at
        z = at.below(k)
        x, y = (at.x, at.y) if mine else (at.ox, at.oy)
        over_x = self.g.at[ch, z, x, at.c, at.y]
        over_y = self.g.at[ch, z, at.x, at.c, y]
        return (
            remote(over_x, over_x, self.p1, (ch, k, 0), at.to_x),
            remote(over_y, over_y, self.p1, (ch, k, 1), at.to_y),
        )

    def p2_copies(self, ch, k, mine=True):
        at = self.at
        z = at.below(k)
        head, tail = pl.ds(0, CUT), pl.ds(CUT, ROWS - CUT)
        if mine:
            over_x = self.g.at[ch, z, at.x, at.c, at.oy, head]
            over_y = self.g.at[ch, z, at.ox, at.c, at.y, tail]
        else:
            over_x = self.g.at[ch, z, at.ox, at.c, at.oy, head]
            over_y = self.g.at[ch, z, at.ox, at.c, at.oy, tail]
        return (
            remote(over_x, over_x, self.p2, (ch, k, 0), at.to_x),
            remote(over_y, over_y, self.p2, (ch, k, 1), at.to_y),
        )

    def c_copy(self, ch, mine=True):
        at = self.at
        ref = self.g.at[ch, :, :, at.c if mine else at.oc]
        return remote(ref, ref, self.cs, (ch,), at.to_c)

    def start_z(self, ch):
        for k in range(1, NZ):
            self.z_copy(ch, k).start()

    def start_own(self, ch):
        for copy in self.p1_copies(ch, 0):
            copy.start()

    def plane(self, ch):
        for k in range(1, NZ):
            self.z_copy(ch, k, False).wait_recv()
            for copy in self.p1_copies(ch, k):
                copy.start()

    def diagonal(self, ch):
        def one(k):
            from_x, from_y = self.p1_copies(ch, k, False)
            over_x, over_y = self.p2_copies(ch, k)
            from_y.wait_recv()
            over_x.start()
            from_x.wait_recv()
            over_y.start()

        loop(NZ, one)

    def cross(self, ch):
        def one(k):
            for copy in self.p2_copies(ch, k, False):
                copy.wait_recv()

        loop(NZ, one)
        self.c_copy(ch).start()

    def arrive(self, ch):
        self.c_copy(ch, False).wait_recv()

    def drain(self, ch):
        for k in range(1, NZ):
            self.z_copy(ch, k).wait_send()

        def one(k):
            for copy in self.p1_copies(ch, k) + self.p2_copies(ch, k):
                copy.wait_send()

        loop(NZ, one)
        self.c_copy(ch).wait_send()


def fold(wide):
    return jnp.concatenate([wide[:, :COLS], wide[:, COLS:]], axis=0)


def pack_weights(refs, put):
    q, k, v, o, inner, outer = refs
    units = [r[...].astype(F32) for r in (q, k, v, o)]
    wide = inner[...].astype(F32)
    units += [wide[:, WIDTH * i : WIDTH * (i + 1)] for i in range(4)]
    for ch in range(4):
        put(ch, jnp.concatenate([fold(units[2 * ch]), fold(units[2 * ch + 1])], axis=0).astype(BF))
    tall = outer[...]
    put(4, tall[:, :COLS])
    put(5, tall[:, COLS:])


def unpack_weights(g, ch, w):
    def one(pair):
        z, x, c = pair // (NX * NC), (pair // NC) % NX, pair % NC
        a = g[ch, z, x, c, 0].astype(F32)
        b = g[ch, z, x, c, 1].astype(F32)
        for unit in range(2):
            base = 48 * unit
            left = jnp.concatenate([a[base : base + 24], b[base : base + 24]], axis=0)
            right = jnp.concatenate([a[base + 24 : base + 48], b[base + 24 : base + 48]], axis=0)
            at = WIDTH * (2 * ch + unit)
            rows = pl.ds(pl.multiple_of(48 * pair, 48), 48)
            w[rows, at : at + COLS] = left.astype(BF)
            w[rows, at + COLS : at + WIDTH] = right.astype(BF)

    loop(GROUP, one)


def spread(gv, vec, ib):
    flat = gv[...].reshape(GROUP * NY * 16, 128)
    row = lax.broadcasted_iota(jnp.int32, (GROUP * NY * 16, WIDTH), 0)
    col = lax.broadcasted_iota(jnp.int32, (GROUP * NY * 16, WIDTH), 1)
    lane = lax.broadcasted_iota(jnp.int32, (128, WIDTH), 0)
    across = lax.broadcasted_iota(jnp.int32, (128, WIDTH), 1)
    first = (row // 16) * 24
    pick = (rem(across, 24) == lane).astype(F32).astype(BF)
    wide = jnp.dot(flat, pick, preferred_element_type=F32)
    wide = jnp.where((col >= first) & (col < first + 24), wide, 0.0)
    vec[...] = jnp.sum(wide.reshape(GROUP * NY, 16, WIDTH), axis=0)
    first = (row // 16) * 96
    for i in range(4):
        pick = (rem(across + WIDTH * i, 96) == lane).astype(F32).astype(BF)
        wide = jnp.dot(flat, pick, preferred_element_type=F32)
        at = col + WIDTH * i
        wide = jnp.where((at >= first) & (at < first + 96) & (rem(row, 16) == 8), wide, 0.0)
        total = jnp.sum(wide, axis=0, keepdims=True)
        ib[:, WIDTH * i : WIDTH * (i + 1)] = jnp.broadcast_to(total, (8, WIDTH))


class Scatter:
    def __init__(self, at, s, r1, rd0, rd1, rx, ry, rz, cs, p2, p1, zs):
        self.at, self.s = at, s
        self.r1, self.rd0, self.rd1, self.rx, self.ry, self.rz = r1, rd0, rd1, rx, ry, rz
        self.cs, self.p2, self.p1, self.zs = cs, p2, p1, zs

    def c_copy(self, ch):
        at = self.at
        return remote(self.s.at[ch, :, :, at.oc], self.r1.at[ch], self.cs, (ch,), at.to_c)

    def p2_copies(self, ch):
        at = self.at
        head, tail = pl.ds(0, CUT), pl.ds(CUT, ROWS - CUT)
        return (
            remote(self.s.at[ch, :, at.ox, at.c, at.oy, head], self.rd0.at[ch], self.p2, (ch, 0), at.to_x),
            remote(self.s.at[ch, :, at.ox, at.c, at.oy, tail], self.rd1.at[ch], self.p2, (ch, 1), at.to_y),
        )

    def p1_copies(self, ch):
        at = self.at
        return (
            remote(self.s.at[ch, :, at.ox, at.c, at.y], self.rx.at[ch], self.p1, (ch, 0), at.to_x),
            remote(self.s.at[ch, :, at.x, at.c, at.oy], self.ry.at[ch], self.p1, (ch, 1), at.to_y),
        )

    def z_copies(self, ch):
        at = self.at
        return [
            remote(self.s.at[ch, at.above(k), at.x, at.c, at.y], self.rz.at[ch, k - 1], self.zs, (ch, k - 1), at.to_z(k))
            for k in range(1, NZ)
        ]

    def start(self, ch):
        self.c_copy(ch).start()

    def add_core(self, ch, x, y):
        def one(z):
            total = self.s[ch, z, x, self.at.c, y].astype(F32) + self.r1[ch, z, x, y].astype(F32)
            self.s[ch, z, x, self.at.c, y] = total.astype(BF)

        loop(NZ, one)

    def core(self, ch):
        at = self.at
        self.c_copy(ch).wait_recv()
        self.add_core(ch, at.ox, at.oy)
        for copy in self.p2_copies(ch):
            copy.start()
        self.add_core(ch, at.ox, at.y)
        self.add_core(ch, at.x, at.oy)
        self.add_core(ch, at.x, at.y)

    def diagonal(self, ch):
        at = self.at
        over_x, over_y = self.p2_copies(ch)
        to_x, to_y = self.p1_copies(ch)
        head, tail = pl.ds(0, CUT), pl.ds(CUT, ROWS - CUT)
        over_x.wait_recv()

        def first(z):
            total = self.s[ch, z, at.x, at.c, at.oy, head].astype(F32) + self.rd0[ch, z].astype(F32)
            self.s[ch, z, at.x, at.c, at.oy, head] = total.astype(BF)

        loop(NZ, first)
        to_y.start()
        over_y.wait_recv()

        def second(z):
            total = self.s[ch, z, at.ox, at.c, at.y, tail].astype(F32) + self.rd1[ch, z].astype(F32)
            self.s[ch, z, at.ox, at.c, at.y, tail] = total.astype(BF)

        loop(NZ, second)
        to_x.start()

    def plane(self, ch):
        at = self.at
        for copy in self.p1_copies(ch):
            copy.wait_recv()

        def one(z):
            total = self.s[ch, z, at.x, at.c, at.y].astype(F32) + self.rx[ch, z].astype(F32)
            total = total + self.ry[ch, z].astype(F32)
            self.s[ch, z, at.x, at.c, at.y] = total.astype(BF)

        loop(NZ, one)
        for copy in self.z_copies(ch):
            copy.start()

    def finish(self, ch):
        at = self.at
        for copy in self.z_copies(ch):
            copy.wait_recv()
        total = self.s[ch, at.z, at.x, at.c, at.y].astype(F32)
        for k in range(NZ - 1):
            total = total + self.rz[ch, k].astype(F32)
        return total

    def drain(self, ch):
        for copy in (self.c_copy(ch), *self.p2_copies(ch), *self.p1_copies(ch), *self.z_copies(ch)):
            copy.wait_send()


def unfold(total, unit):
    base = 48 * unit
    return jnp.concatenate([total[base : base + 24], total[base + 24 : base + 48]], axis=1)


class VectorScatter:
    def __init__(self, at, s, rc, rx, ry, rz, sems):
        self.at, self.s = at, s
        self.rc, self.rx, self.ry, self.rz, self.sems = rc, rx, ry, rz, sems
        at = self.at
        self.cc = remote(s.at[:, :, at.oc], rc, sems, 0, at.to_c)
        self.xx = remote(s.at[:, at.ox, at.c], rx, sems, 1, at.to_x)
        self.yy = remote(s.at[:, at.x, at.c, at.oy], ry, sems, 2, at.to_y)
        self.zz = [
            remote(s.at[at.above(k), at.x, at.c, at.y], rz.at[k - 1], sems, 2 + k, at.to_z(k)) for k in range(1, NZ)
        ]

    def start(self):
        self.cc.start()

    def core(self):
        self.cc.wait_recv()
        self.s[:, :, self.at.c] = self.s[:, :, self.at.c] + self.rc[...]
        self.xx.start()

    def over_x(self):
        at = self.at
        self.xx.wait_recv()
        self.s[:, at.x, at.c] = self.s[:, at.x, at.c] + self.rx[...]
        self.yy.start()

    def over_y(self):
        at = self.at
        self.yy.wait_recv()
        self.s[:, at.x, at.c, at.y] = self.s[:, at.x, at.c, at.y] + self.ry[...]
        for copy in self.zz:
            copy.start()

    def finish(self):
        at = self.at
        for copy in self.zz:
            copy.wait_recv()
        return self.s[at.z, at.x, at.c, at.y] + self.rz[0] + self.rz[1] + self.rz[2]

    def drain(self):
        for copy in [self.cc, self.xx, self.yy] + self.zz:
            copy.wait_send()


def own_part(value, stride):
    if stride == 1:
        return value
    whole = lax.all_gather(value, ("dp", "blk"), axis=0, tiled=True)
    rows = whole.shape[0] // (GROUP * NY)
    index = (lax.axis_index("dp") // stride) * NY + lax.axis_index("blk")
    return lax.dynamic_slice_in_dim(whole, index * rows, rows, axis=0)


def fine_part(value, stride):
    if stride == 1:
        return value
    index = (lax.axis_index("dp") // stride) * NY + lax.axis_index("blk")
    rows = value.shape[0]
    whole = jnp.zeros((rows * GROUP * NY,) + value.shape[1:], value.dtype)
    whole = lax.dynamic_update_slice_in_dim(whole, value, index * rows, axis=0)
    return lax.psum_scatter(whole, ("dp", "blk"), scatter_dimension=0, tiled=True)


def product(left, right):
    return jnp.dot(left, right, preferred_element_type=F32)


def product_left(left, right):
    return lax.dot_general(left, right, (((0,), (0,)), ((), ())), preferred_element_type=F32)


def product_right(left, right):
    return lax.dot_general(left, right, (((1,), (1,)), ((), ())), preferred_element_type=F32)


def tile(i, size):
    return pl.ds(pl.multiple_of(i * size, size), size)


def mean(values):
    return jnp.mean(values, axis=-1, keepdims=True)


def column(values):
    return jnp.sum(values, axis=0, keepdims=True)


def gather_vectors(vg, ibg, sv):
    owners = GROUP * NY

    def pieces(values, pick):
        high = values.astype(BF)
        rest = (values - high.astype(F32)).astype(BF)
        return product(high, pick) + product(rest, pick)

    def grids(shape):
        return [lax.broadcasted_iota(jnp.int32, shape, i) for i in range(len(shape))]

    across, lane = grids((WIDTH, 128))
    device, row, col = grids((owners, 16, WIDTH))
    pick = ((rem(across, 24) == lane) & (lane < 24)).astype(F32).astype(BF)
    first = device * 24
    wide = jnp.where((col >= first) & (col < first + 24), vg[...][None], 0.0)
    total = pieces(wide.reshape(owners * 16, WIDTH), pick)
    first = device * 96
    for i in range(4):
        pick = ((rem(across + WIDTH * i, 96) == lane) & (lane < 96)).astype(F32).astype(BF)
        at = col + WIDTH * i
        values = ibg[0:1, WIDTH * i : WIDTH * (i + 1)][None]
        wide = jnp.where((at >= first) & (at < first + 96) & (row == 8), values, 0.0)
        total = total + pieces(wide.reshape(owners * 16, WIDTH), pick)
    sv[...] = total.reshape(sv.shape)


QB, VB, OB, G1, S1, UB, G2, S2 = range(8)


def layer_kernel(
    stride,
    q, k, v, o, inner, outer, small, hidden, grad, mask,
    out, igrad, dq, dk, dv, do, di, du, dsmall, saved,
    g, gv, wd, u, page, cot, dead, hid, qkv, outp, xt, hidt, ctxt,
    n1, inv1, acc1, acc2, dst, bias, vec, ib, vg, ibg,
    sv, r1, rd0, rd1, rx, ry, rz, vc, vx, vy, vz,
    zs, zr, p1s, p1r, p2s, p2r, cs, cr, vs, vr, es, er,
    css, csr, q2s, q2r, q1s, q1r, zss, zsr, ws, wr, loads, saves,
):
    at = Place(stride)
    gather = Gather(at, g, (zs, zr), (p1s, p1r), (p2s, p2r), (cs, cr))
    scatter = Scatter(
        at, g, r1, rd0, rd1, rx, ry, rz, (css, csr), (q2s, q2r), (q1s, q1r), (zss, zsr)
    )
    vector = VectorScatter(at, sv, vc, vx, vy, vz, (ws, wr))

    def put(ch, value):
        g[ch, at.z, at.x, at.c, at.y] = value

    pack_weights((q, k, v, o, inner, outer), put)
    gv[at.z, at.x, at.c, at.y] = small[...]
    own = pl.ds(pl.multiple_of(at.y * 256, 256), 256)
    theirs = pl.ds(pl.multiple_of(at.oy * 256, 256), 256)
    local = [
        pltpu.make_async_copy(hidden.at[at.y], page.at[own], loads.at[0]),
        pltpu.make_async_copy(grad.at[at.y], cot.at[own], loads.at[1]),
    ]
    for copy in local:
        copy.start()
    at.greet()

    ve, ee = (vs, vr), (es, er)
    swaps = [
        remote(hidden.at[at.oy], page.at[own], ee, 0, at.to_y),
        remote(mask.at[at.oy], dead.at[at.y], ee, 1, at.to_y),
        remote(grad.at[at.oy], cot.at[own], ee, 2, at.to_y),
        remote(outp.at[theirs], out.at[at.y], ee, 3, at.to_y),
        remote(cot.at[theirs], igrad.at[at.y], ee, 4, at.to_y),
    ]
    mine = gv.at[at.z, at.x, at.c, at.y]
    vzs = [remote(mine, mine, ve, kk - 1, at.to_z(kk)) for kk in range(1, NZ)]
    for copy in vzs:
        copy.start()
    swaps[0].start()
    swaps[1].start()
    gather.start_z(0)
    gather.start_own(0)
    gather.start_z(1)
    gather.start_own(1)
    for copy in vzs:
        copy.wait_recv()
    line = gv.at[:, at.x, at.c, at.y]
    vxs = remote(line, line, ve, 3, at.to_x)
    vxs.start()
    loop(CHUNKS - 2, lambda i: gather.start_z(i + 2))
    dead[at.y] = mask[at.y]
    vxs.wait_recv()
    pairs = gv.at[:, :, at.c, at.y]
    vys = remote(pairs, pairs, ve, 4, at.to_y)
    vys.start()
    gather.plane(0)
    vys.wait_recv()
    core = gv.at[:, :, at.c]
    vcs = remote(core, core, ve, 5, at.to_c)
    vcs.start()

    gather.start_own(2)
    gather.plane(1)
    gather.diagonal(0)
    vcs.wait_recv()
    spread(gv, vec, ib)
    gather.start_own(3)
    gather.plane(2)
    gather.diagonal(1)
    gather.cross(0)
    for copy in local:
        copy.wait()
    swaps[0].wait_recv()
    swaps[1].wait_recv()

    def turn(i):
        xt[tile(i, 256), :] = page[:, tile(i, 256)].T

    loop(3, turn)
    for half in range(2):
        bias[256 * half : 256 * half + 256] = jnp.broadcast_to(dead[half, 0:1].T, (256, 128))
    gather.start_own(4)
    gather.plane(3)
    gather.arrive(0)
    unpack_weights(g, 0, wd)

    def queries(i):
        cols = tile(i, 256)
        value = product(page[...], wd[:, cols]) + vec[QB : QB + 1, cols]
        qkv[:, cols] = (value.astype(BF).astype(F32) * 0.125).astype(BF)

    def keys(i):
        cols = tile(i + 3, 256)
        qkv[:, cols] = product(page[...], wd[:, cols]).astype(BF)

    def vals(i):
        cols = tile(i + 6, 256)
        value = product(page[...], wd[:, cols]) + vec[VB : VB + 1, tile(i, 256)]
        qkv[:, cols] = value.astype(BF)

    loop(3, queries)
    loop(3, keys)
    gather.diagonal(2)
    gather.cross(1)
    gather.start_own(5)
    gather.plane(4)
    gather.arrive(1)
    unpack_weights(g, 1, wd)
    loop(3, vals)
    lane = lax.broadcasted_iota(jnp.int32, (512, 128), 1)
    sides = (lane < 64, lane >= 64)

    def side(value, which):
        return jnp.where(sides[which], value.astype(F32), 0.0).astype(BF)

    def save(pair):
        cols = tile(pair, 1024)
        return pltpu.make_async_copy(u.at[:, cols], saved.at[:, cols], saves.at[pair])

    def attend(pair):
        at_q, at_k, at_v = tile(pair, 128), tile(pair + 6, 128), tile(pair + 12, 128)
        k2, v2 = qkv[:, at_k], qkv[:, at_v]
        total = jnp.zeros((128, 512), F32)
        for a in range(2):
            ka, va = side(k2, a), side(v2, a)
            for h in range(2):
                q2 = qkv[256 * h : 256 * h + 256, at_q]
                s = product_right(ka, q2) + jnp.concatenate([bias[...], bias[...]], axis=1)
                e = jnp.exp(s - jnp.max(s, axis=0, keepdims=True))
                p = e * (1.0 / jnp.sum(e, axis=0, keepdims=True))
                cols = pl.ds(pl.multiple_of(1024 * pair + 512 * a + 256 * h, 256), 256)
                u[:, cols] = p.astype(BF)
            cols = pl.ds(pl.multiple_of(1024 * pair + 512 * a, 512), 512)
            total = total + product_left(va, u[:, cols])
        ctxt[tile(pair, 128), :] = total.astype(BF)
        outp[:, tile(pair, 128)] = total.T.astype(BF)
        save(pair).start()

    def steps(*table):
        def run(i):
            for index, work in enumerate(table):
                pl.when(i == index)(work)

        return run

    def attend_and(table):
        def run(i):
            attend(i)
            steps(*table)(i)

        return run

    def start_cot():
        swaps[2].start()
        gather.cross(2)

    loop(
        6,
        attend_and(
            (
                lambda: gather.diagonal(3),
                start_cot,
                lambda: gather.plane(5),
                lambda: gather.diagonal(4),
                lambda: gather.cross(3),
            )
        ),
    )

    def attended(i):
        cols = tile(i, 256)
        value = product(outp[...], wd[:, tile(i + 9, 256)]) + vec[OB : OB + 1, cols]
        acc1[:, cols] = page[:, cols].astype(F32) + value

    loop(3, attended)
    gather.diagonal(5)
    gather.cross(4)

    def first_norm(i):
        rows = tile(i, 64)
        joined = acc1[rows, :]
        center = joined - mean(joined)
        inverse = lax.rsqrt(mean(center * center) + EPSILON)
        normed = center * inverse
        n1[rows, :] = normed
        inv1[rows, :] = jnp.broadcast_to(inverse, (64, 128))
        hid[rows, :] = (normed * vec[G1 : G1 + 1] + vec[S1 : S1 + 1]).astype(BF)

    loop(8, first_norm)

    def turn_hidden(i):
        hidt[tile(i, 256), :] = hid[:, tile(i, 256)].T

    loop(3, turn_hidden)
    gather.arrive(2)
    unpack_weights(g, 2, wd)
    gather.arrive(3)
    unpack_weights(g, 3, wd)
    loop(6, lambda i: save(i).wait())
    gather.cross(5)

    def feed(i):
        cols = tile(i, 384)
        weight = wd[:, pl.ds(pl.multiple_of(4 * WIDTH + 384 * i, 384), 384)]
        acc1[:, 0:384] = product(hid[...], weight) + ib[0:1, cols]

        def one(r):
            rows = tile(r, 64)
            value = acc1[rows, 0:384]
            cdf = 0.5 + 0.5 * lax.erf(value * 0.7071067811865476)
            density = 0.3989422804014327 * jnp.exp(-0.5 * value * value)
            u[rows, cols] = (value * cdf).astype(BF)
            u[rows, pl.ds(pl.multiple_of(3072 + 384 * i, 384), 384)] = (cdf + value * density).astype(BF)

        loop(8, one)

    loop(8, feed)
    for half in range(2):
        gather.arrive(4 + half)
        cols = slice(COLS * half, COLS * half + COLS)
        weight = g[4 + half].reshape(8 * COLS, COLS)
        acc1[:, cols] = product(u[:, 0:3072], weight)
    swaps[2].wait_recv()

    vg[...] = jnp.zeros_like(vg)

    def second_norm(i):
        rows = tile(i, 64)
        second = hid[rows, :].astype(F32) + (acc1[rows, :] + vec[UB : UB + 1])
        center = second - mean(second)
        inverse = lax.rsqrt(mean(center * center) + EPSILON)
        normed = center * inverse
        gain = vec[G2 : G2 + 1]
        outp[rows, :] = (normed * gain + vec[S2 : S2 + 1]).astype(BF)
        dy = cot[rows, :].astype(F32)
        vg[G2 : G2 + 1] += column(dy * normed)
        vg[S2 : S2 + 1] += column(dy)
        scaled = dy * gain
        back = inverse * (scaled - mean(scaled) - normed * mean(scaled * normed))
        acc2[rows, :] = back
        low = back.astype(BF)
        page[rows, :] = low
        vg[UB : UB + 1] += column(low.astype(F32))

    loop(8, second_norm)
    swaps[3].start()
    keep = pltpu.make_async_copy(outp.at[own], out.at[at.y], loads.at[0])
    keep.start()

    low = page
    loop(CHUNKS, gather.drain)

    def outer_grad(i):
        z, x = i // 2, rem(i, 2)
        value = product_left(u[:, tile(i, 384)], low[...]).astype(BF)
        for half in range(2):
            part = value[:, COLS * half : COLS * half + COLS]
            g[half, z, x] = part.reshape(NC, NY, ROWS, COLS)

    loop(8, outer_grad)
    scatter.start(0)
    scatter.start(1)

    def load(part):
        cols = pl.ds(3072 * part, 3072)
        return pltpu.make_async_copy(saved.at[:, cols], u.at[:, cols], loads.at[1])

    load(0).start()

    def inner_back(i):
        z, x = i // 2, rem(i, 2)
        value = product_right(low[:, 0:COLS], g[4, z, x].reshape(COLS, COLS))
        value = value + product_right(low[:, COLS:], g[5, z, x].reshape(COLS, COLS))
        cols = pl.ds(pl.multiple_of(3072 + 384 * i, 384), 384)
        value = (value * u[:, cols].astype(F32)).astype(BF)
        u[:, cols] = value
        total = column(value.astype(F32))
        ibg[:, tile(i, 384)] = jnp.broadcast_to(total, (8, 384))

    loop(8, inner_back)
    scatter.core(0)

    def weight_grad(slot, unit, left, right):
        def one(i):
            value = product(left[tile(i, 384), :], right)
            value = value.reshape(16, 24, WIDTH)
            value = jnp.concatenate([value[:, :, :COLS], value[:, :, COLS:]], axis=1).astype(BF)
            g[slot, pl.ds(2 * i, 2), :, :, :, 48 * unit : 48 * unit + 48, :] = value.reshape(
                2, NX, NC, NY, 48, COLS
            )

        loop(2, one)

    def inner_grad(unit):
        right = u[:, 3072 + WIDTH * unit : 3072 + WIDTH * (unit + 1)]
        weight_grad(2 + unit // 2, unit % 2, hidt, right)

    inner_grad(0)
    inner_grad(1)
    scatter.start(2)
    scatter.core(1)
    inner_grad(2)
    inner_grad(3)
    scatter.start(3)
    scatter.diagonal(0)

    def hidden_back(i):
        cols = tile(i, 256)
        acc2[:, cols] = acc2[:, cols] + product_right(u[:, 3072:6144], wd[cols, 4 * WIDTH :])

    loop(3, hidden_back)
    load(0).wait()
    load(1).start()
    scatter.core(2)
    scatter.diagonal(1)

    def first_back(i):
        rows = tile(i, 64)
        up = acc2[rows, :]
        normed = n1[rows, :]
        vg[G1 : G1 + 1] += column(up * normed)
        vg[S1 : S1 + 1] += column(up)
        scaled = up * vec[G1 : G1 + 1]
        inverse = inv1[rows, 0:1]
        back = inverse * (scaled - mean(scaled) - normed * mean(scaled * normed))
        acc2[rows, :] = back
        short = back.astype(BF)
        low[rows, :] = short
        vg[OB : OB + 1] += column(short.astype(F32))

    loop(8, first_back)
    weight_grad(4, 1, ctxt, low[...])

    def context_back(i):
        cols = tile(i, 256)
        hid[:, cols] = product_right(low[...], wd[cols, 3 * WIDTH : 4 * WIDTH]).astype(BF)

    loop(3, context_back)
    scatter.plane(0)
    load(1).wait()

    def attend_back(pair):
        at_q, at_k, at_v = tile(pair, 128), tile(pair + 6, 128), tile(pair + 12, 128)
        q2, k2, v2, c2 = qkv[:, at_q], qkv[:, at_k], qkv[:, at_v], hid[:, at_q]
        dqt = jnp.zeros((128, 512), F32)
        dk2 = jnp.zeros((512, 128), F32)
        dv2 = jnp.zeros((512, 128), F32)
        for a in range(2):
            va = side(v2, a)
            for h in range(2):
                cols = pl.ds(pl.multiple_of(1024 * pair + 512 * a + 256 * h, 256), 256)
                p = u[:, cols].astype(F32)
                d = product_right(va, c2[256 * h : 256 * h + 256])
                delta = jnp.sum(p * d, axis=0, keepdims=True)
                dst[:, 256 * h : 256 * h + 256] = (p * (d - delta)).astype(BF)
            cols = pl.ds(pl.multiple_of(1024 * pair + 512 * a, 512), 512)
            dv2 = dv2 + product(u[:, cols], side(c2, a))
            dk2 = dk2 + product(dst[...], side(q2, a))
            dqt = dqt + product_left(side(k2, a), dst[...])
        qkv[:, at_q] = (dqt.T * 0.125).astype(BF)
        qkv[:, at_k] = dk2.astype(BF)
        qkv[:, at_v] = dv2.astype(BF)

    def back_and(table):
        def run(i):
            attend_back(i)
            steps(*table)(i)

        return run

    loop(
        6,
        back_and(
            (
                lambda: scatter.diagonal(2),
                lambda: scatter.core(3),
                lambda: scatter.plane(1),
                lambda: scatter.diagonal(3),
                lambda: scatter.plane(2),
            )
        ),
    )
    weight_grad(4, 0, xt, qkv[:, 2 * WIDTH : 3 * WIDTH])
    scatter.start(4)
    weight_grad(5, 0, xt, qkv[:, 0:WIDTH])
    scatter.core(4)
    weight_grad(5, 1, xt, qkv[:, WIDTH : 2 * WIDTH])
    scatter.start(5)

    def sums(i):
        rows = tile(i, 64)
        vg[QB : QB + 1] += column(qkv[rows, 0:WIDTH].astype(F32))
        vg[VB : VB + 1] += column(qkv[rows, 2 * WIDTH : 3 * WIDTH].astype(F32))

    loop(8, sums)
    gather_vectors(vg, ibg, sv)
    vector.start()
    scatter.diagonal(4)
    scatter.core(5)
    scatter.plane(3)
    vector.core()

    def input_back(i):
        cols = tile(i, 256)
        value = acc2[:, cols] + product_right(qkv[...], wd[cols, 0 : 3 * WIDTH])
        cot[:, cols] = value.astype(BF)

    loop(3, input_back)
    vector.over_x()
    scatter.diagonal(5)
    swaps[4].start()
    keep_in = pltpu.make_async_copy(cot.at[own], igrad.at[at.y], loads.at[1])
    keep_in.start()
    scatter.plane(4)
    vector.over_y()

    outs = (q, k, v, o)
    targets = (dq, dk, dv, do)

    def finish(n):
        total = scatter.finish(n)
        if n < 2:
            du[:, COLS * n : COLS * n + COLS] = total
        elif n < 4:
            for unit in range(2):
                index = 2 * (n - 2) + unit
                di[:, WIDTH * index : WIDTH * (index + 1)] = unfold(total, unit)
        else:
            first, second = (dv, do) if n == 4 else (dq, dk)
            first[...] = unfold(total, 0)
            second[...] = unfold(total, 1)

    for n in range(4):
        finish(n)
    scatter.plane(5)
    dsmall[...] = vector.finish()
    finish(4)
    finish(5)

    keep.wait()
    keep_in.wait()
    swaps[3].wait_recv()
    swaps[4].wait_recv()
    loop(CHUNKS, scatter.drain)
    vector.drain()
    for copy in vzs + [vxs, vys, vcs] + swaps:
        copy.wait_send()


def layer_call(stride, args):
    vmem = pl.BlockSpec(memory_space=pltpu.VMEM)
    hbm = pl.BlockSpec(memory_space=pl.ANY)
    dma = pltpu.SemaphoreType.DMA

    def shape(*dims, kind=F32):
        return jax.ShapeDtypeStruct(dims, kind)

    tokens = [shape(2, 256, WIDTH, kind=BF)] * 2
    grads = [shape(24, WIDTH)] * 4 + [shape(24, 4 * WIDTH), shape(96, WIDTH), shape(16, 128)]

    def low(*dims):
        return pltpu.VMEM(dims, BF)

    def full(*dims):
        return pltpu.VMEM(dims, F32)

    def pair(*dims):
        return [dma(dims), dma(dims)]

    return pl.pallas_call(
        partial(layer_kernel, stride),
        out_shape=tuple(tokens + grads + [shape(512, 12 * 512, kind=BF)]),
        in_specs=[vmem] * 7 + [hbm, hbm, vmem],
        out_specs=tuple([hbm] * 2 + [vmem] * len(grads) + [hbm]),
        scratch_shapes=[
            low(CHUNKS, NZ, NX, NC, NY, ROWS, COLS),
            low(NZ, NX, NC, NY, 16, 128),
            low(WIDTH, 8 * WIDTH),
            low(512, 12 * 512),
            low(512, WIDTH),
            low(512, WIDTH),
            full(2, 8, 256),
            low(512, WIDTH),
            low(512, 3 * WIDTH),
            low(512, WIDTH),
            low(WIDTH, 512),
            low(WIDTH, 512),
            low(WIDTH, 512),
            full(512, WIDTH),
            full(512, 128),
            full(512, WIDTH),
            full(512, WIDTH),
            low(512, 512),
            full(512, 128),
            full(16, WIDTH),
            full(8, 4 * WIDTH),
            full(16, WIDTH),
            full(8, 4 * WIDTH),
            full(NZ, NX, NC, NY, 16, 128),
            low(CHUNKS, NZ, NX, NY, ROWS, COLS),
            low(CHUNKS, NZ, CUT, COLS),
            low(CHUNKS, NZ, ROWS - CUT, COLS),
            low(CHUNKS, NZ, ROWS, COLS),
            low(CHUNKS, NZ, ROWS, COLS),
            low(CHUNKS, NZ - 1, ROWS, COLS),
            full(NZ, NX, NY, 16, 128),
            full(NZ, NY, 16, 128),
            full(NZ, 16, 128),
            full(NZ - 1, 16, 128),
            *pair(CHUNKS, NZ - 1),
            *pair(CHUNKS, NZ, 2),
            *pair(CHUNKS, NZ, 2),
            *pair(CHUNKS),
            *pair(6),
            *pair(5),
            *pair(CHUNKS),
            *pair(CHUNKS, 2),
            *pair(CHUNKS, 2),
            *pair(CHUNKS, NZ - 1),
            *pair(6),
            dma((2,)),
            dma((6,)),
        ],
        compiler_params=pltpu.CompilerParams(
            collective_id=0, has_side_effects=True, vmem_limit_bytes=VMEM_LIMIT
        ),
        name="layer",
    )(*args)


def body(
    stride,
    hidden_in,
    page_lengths,
    pad_mask,
    query_weight,
    query_bias,
    key_weight,
    value_weight,
    value_bias,
    output_weight,
    output_bias,
    first_gain,
    first_shift,
    inner_weight,
    inner_bias,
    outer_weight,
    outer_bias,
    second_gain,
    second_shift,
    out_grad,
):
    coarse = partial(own_part, stride=stride)
    fine = partial(fine_part, stride=stride)
    place = lax.axis_index("blk")
    segment = hidden_in.shape[1]
    positions = place * segment + jnp.arange(segment, dtype=jnp.int32)
    live = (positions[None, :] < page_lengths[:, None]) & (pad_mask == 1)
    mask = jnp.where(live, 0.0, NEG_FILL).astype(F32)
    mask = jnp.broadcast_to(mask[:, None, :], (2, 8, segment))
    vectors = (
        query_bias, value_bias, output_bias, first_gain, first_shift, outer_bias, second_gain, second_shift,
    )
    small = jnp.stack([coarse(v) for v in vectors])
    small = jnp.concatenate(
        [
            jnp.pad(small, ((0, 0), (0, 104))),
            jnp.pad(coarse(inner_bias)[None, :], ((0, 7), (0, 32))),
        ]
    )
    weights = [
        coarse(v) for v in (query_weight, key_weight, value_weight, output_weight, inner_weight, outer_weight)
    ]
    output, input_grad, dq, dk, dv, do, di, du, dsmall, _ = layer_call(
        stride, (*weights, small, hidden_in, out_grad, mask)
    )
    qbg, vbg, obg, g1g, s1g, ubg, g2g, s2g = [fine(dsmall[i, :24]) for i in range(8)]
    return (
        output,
        input_grad,
        fine(dq),
        qbg,
        fine(dk),
        fine(dv),
        vbg,
        fine(do),
        obg,
        g1g,
        s1g,
        fine(di),
        fine(dsmall[8, :96]),
        fine(du),
        ubg,
        g2g,
        s2g,
    )


def solution(mesh):
    stride = mesh.shape["dp"] // GROUP
    row = P(("dp", "blk"))
    mat = P(("dp", "blk"), None)
    tok = P("dp", "blk", None)
    in_specs = (
        tok, P("dp"), P("dp", "blk"), mat, row, mat, mat, row, mat, row, row, row, mat, row, mat, row, row, row, tok,
    )
    out_specs = (
        tok, tok, mat, row, mat, mat, row, mat, row, row, row, mat, row, mat, row, row, row,
    )
    return jax.shard_map(
        partial(body, stride), mesh=mesh, in_specs=in_specs, out_specs=out_specs, check_vma=False
    )
```

profile of v0, /device:TPU:0, one launch (start us, length us, event | category | flops | bytes accessed | tf_op | source)
XLA Modules:
  0.0 208.6 jit_solution(18012015354694332642)
XLA Ops:
  0.7 0.8 and_select_fusion
  1.4 0.8 stack.35
  2.2 1.3 fusion.2.small
  3.5 0.6 broadcast_in_dim.22.mask
  4.1 188.2 %layer.1 = (bf16[2,256,768]{2,1,0:T(8,128)(2,1)}, bf16[2,256,768]{2,1,0:T(8,128)(2,1)}, f32[24,768]{1,0:T(8,128)}, f32[24,768]{1,0:T(8,128)}, f32[24,768]{1,0:T(...) custom-call(bf16[24,768]{1,0:T(8,128)(2,1)} %q.1, ...), custom_call_target="tpu_custom_call" | custom-call | tf_op jit(solution)/shard_map/layer/pallas_call | solution.py:935
  192.3 1.2 slice_bitcast_fusion.3
  193.5 1.5 slice_bitcast_fusion
  195.0 2.1 copy.44
  197.0 2.1 copy.45
  199.1 1.5 copy.46
  200.6 1.5 copy.47
  202.1 1.5 copy.48
  203.7 1.5 copy.49
  205.2 1.7 copy.50
  206.9 1.7 copy.51
  (1 shorter events, 0.0 us)
where the time goes:
time: 209 us
  Pallas kernels  188 us (90%)
  local copies, waits for them, and re-layouts  17.7 us (8%)
    pallas_call x1, Pallas kernels, layer_call(): pl.pallas_call(partial(layer_kernel, stride), out_shape=tuple(tokens + gr...  188 us
    unnamed x8, local copies, waits for them, and re-layouts  13.6 us

commit v1 on v0

--- a/solution.py
+++ b/solution.py
@@ -15,10 +15,40 @@
 GROUP = NZ * NX * NC
 CHUNKS = 6
 ROWS, COLS = 96, 384
+LATE = 5
 CUT = 64
 WIDTH = 768
+FINE = (4, 5)
 BF, F32 = jnp.bfloat16, jnp.float32
 VMEM_LIMIT = 62 * 2**20
+
+FORWARD = (
+    "own 1", "own 5", "vector_z", "z 0", "turn 1 0", "page", "own 2", "vector_x", "own 0", "turn 5 0",
+    "plane 0 3", "z 1", "plane 0 1", "page_wait", "z 2", "plane 1 3", "z 4", "plane 1 1", "plane 1 2",
+    "turn 0 3", "plane 0 2", "vector_y", "turn 0 1", "turn 0 0", "turn 1 3", "turn 1 2", "z 3", "turn 0 2",
+    "turn 1 1", "plane 4 2", "plane 2 3", "late_z", "cross 0", "vector_c", "plane 2 1", "own 3", "plane 2 2",
+    "cross 1", "vector_wait", "arrive 0", "plane 3 1", "prepare", "unpack 0", "plane 3 3", "own 4", "turn 2 3",
+    "turn 2 1", "arrive 1", "unpack 1", "queries_keys", "turn 2 2", "plane 3 2", "turn 2 0", "values",
+    "turn 3 1", "attend 0", "attend 1", "plane 4 3", "attend 2", "attend 3", "turn 3 0", "plane 4 1", "cross 2",
+    "turn 3 3", "attend 4", "turn 3 2", "grad", "turn 4 0", "attend 5", "arrive 2", "after_attention",
+    "unpack 2", "cross 3", "feed 0", "turn 4 3", "feed 1", "turn 4 2", "feed 2", "late_cross", "arrive 3",
+    "turn 4 1", "feed 3", "unpack 3", "feed_on 4", "cross 4", "feed_on 5", "feed_on 6", "feed_on 7", "arrive 4",
+    "arrive 5", "outer 0", "grad_wait", "outer 1",
+)
+BACKWARD = (
+    "out", "outer_first", "start 1", "outer_second", "inner_back 0", "inner_back 1", "start 0", "core 1",
+    "inner_back 2", "inner_back 3", "inner_back 4", "early_core", "inner_back 5", "inner_back 6", "diagonal 1",
+    "inner_back 7", "inner_grad 0", "inner_grad 1", "start 2", "inner_grad 2", "inner_grad 3", "hidden_back 0",
+    "hidden_back 1", "core 2", "start 3", "hidden_back 2", "first_back", "context_back", "core 3",
+    "attend_back 0", "diagonal 2", "attend_back 1", "attend_back 2", "diagonal 3", "attend_back 3",
+    "attend_back 4", "output_grad", "attend_back 5", "query_grad", "plane 1", "value_grad", "start 4",
+    "key_grad", "early_plane", "sums", "start 5", "gather_vectors", "vector", "core 4", "plane 2",
+    "vector_core", "core 5", "plane 3", "diagonal 4 2", "diagonal 4 0", "finish 1", "input_back 0",
+    "diagonal 4 1", "vector_x", "diagonal 4 3", "vector_y", "diagonal 5 2", "diagonal 5 0", "plane 4 2",
+    "diagonal 5 1", "input_back 1", "early_diagonal", "finish 2", "plane 4 0", "diagonal 5 3", "plane 4 1",
+    "finish 3", "input_back 2", "vector_finish", "grad", "plane 5 2", "plane 5 1", "plane 4 3", "plane 5 3",
+    "finish 4", "plane 5 0", "finish 0", "finish 5",
+)
 
 
 def rem(a, b):
@@ -61,12 +91,15 @@
     def to_c(self):
         return self.dev(self.z, self.x, self.oc, self.y)
 
-    def greet(self):
-        barrier = pltpu.get_barrier_semaphore()
+    def hail(self):
         partners = [self.to_z(k) for k in range(1, NZ)] + [self.to_x, self.to_y, self.to_c]
         for who in partners:
-            pl.semaphore_signal(barrier, inc=1, device_id=who, device_id_type=pl.DeviceIdType.MESH)
-        pl.semaphore_wait(barrier, len(partners))
+            pl.semaphore_signal(
+                pltpu.get_barrier_semaphore(), inc=1, device_id=who, device_id_type=pl.DeviceIdType.MESH
+            )
+
+    def meet(self):
+        pl.semaphore_wait(pltpu.get_barrier_semaphore(), NZ + 2)
 
 
 def remote(src, dst, sems, index, who):
@@ -139,22 +172,18 @@
         for copy in self.p1_copies(ch, 0):
             copy.start()
 
-    def plane(self, ch):
-        for k in range(1, NZ):
-            self.z_copy(ch, k, False).wait_recv()
-            for copy in self.p1_copies(ch, k):
-                copy.start()
-
-    def diagonal(self, ch):
-        def one(k):
-            from_x, from_y = self.p1_copies(ch, k, False)
-            over_x, over_y = self.p2_copies(ch, k)
-            from_y.wait_recv()
-            over_x.start()
-            from_x.wait_recv()
-            over_y.start()
-
-        loop(NZ, one)
+    def plane(self, ch, k):
+        self.z_copy(ch, k, False).wait_recv()
+        for copy in self.p1_copies(ch, k):
+            copy.start()
+
+    def turn(self, ch, k):
+        from_x, from_y = self.p1_copies(ch, k, False)
+        over_x, over_y = self.p2_copies(ch, k)
+        from_y.wait_recv()
+        over_x.start()
+        from_x.wait_recv()
+        over_y.start()
 
     def cross(self, ch):
         def one(k):
@@ -164,6 +193,22 @@
         loop(NZ, one)
         self.c_copy(ch).start()
 
+    def late_copy(self, k, mine=True):
+        at = self.at
+        ref = self.g.at[LATE, at.z if mine else at.below(k), :, at.c]
+        return remote(ref, ref, self.zs, (LATE, k - 1), at.to_z(k))
+
+    def late_z(self):
+        for copy in self.p2_copies(LATE, 0, False):
+            copy.wait_recv()
+        for k in range(1, NZ):
+            self.late_copy(k).start()
+
+    def late_cross(self):
+        for k in range(1, NZ):
+            self.late_copy(k, False).wait_recv()
+        self.c_copy(LATE).start()
+
     def arrive(self, ch):
         self.c_copy(ch, False).wait_recv()
 
@@ -177,6 +222,12 @@
 
         loop(NZ, one)
         self.c_copy(ch).wait_send()
+
+    def late_drain(self):
+        for k in range(1, NZ):
+            self.late_copy(k).wait_send()
+        for copy in (*self.p1_copies(LATE, 0), *self.p2_copies(LATE, 0), self.c_copy(LATE)):
+            copy.wait_send()
 
 
 def fold(wide):
@@ -213,29 +264,30 @@
 
 
 def spread(gv, vec, ib):
-    flat = gv[...].reshape(GROUP * NY * 16, 128)
-    row = lax.broadcasted_iota(jnp.int32, (GROUP * NY * 16, WIDTH), 0)
-    col = lax.broadcasted_iota(jnp.int32, (GROUP * NY * 16, WIDTH), 1)
+    owners = GROUP * NY
+    parts = gv[...].astype(F32).reshape(owners, 16, 128)
+    across = lax.broadcasted_iota(jnp.int32, (128, WIDTH), 1)
     lane = lax.broadcasted_iota(jnp.int32, (128, WIDTH), 0)
-    across = lax.broadcasted_iota(jnp.int32, (128, WIDTH), 1)
-    first = (row // 16) * 24
-    pick = (rem(across, 24) == lane).astype(F32).astype(BF)
-    wide = jnp.dot(flat, pick, preferred_element_type=F32)
-    wide = jnp.where((col >= first) & (col < first + 24), wide, 0.0)
-    vec[...] = jnp.sum(wide.reshape(GROUP * NY, 16, WIDTH), axis=0)
-    first = (row // 16) * 96
+    device = lax.broadcasted_iota(jnp.int32, (owners, 8, WIDTH), 0)
+    col = lax.broadcasted_iota(jnp.int32, (owners, 8, WIDTH), 2)
+
+    def placed(flat, size, start):
+        pick = (rem(across + start, size) == lane).astype(F32).astype(BF)
+        wide = jnp.dot(flat, pick, preferred_element_type=F32).reshape(owners, 8, WIDTH)
+        first = device * size - start
+        return jnp.sum(jnp.where((col >= first) & (col < first + size), wide, 0.0), axis=0)
+
+    vec[...] = placed(parts[:, 0:8].reshape(owners * 8, 128).astype(BF), 24, 0)
+    flat = parts[:, 8:16].reshape(owners * 8, 128).astype(BF)
     for i in range(4):
-        pick = (rem(across + WIDTH * i, 96) == lane).astype(F32).astype(BF)
-        wide = jnp.dot(flat, pick, preferred_element_type=F32)
-        at = col + WIDTH * i
-        wide = jnp.where((at >= first) & (at < first + 96) & (rem(row, 16) == 8), wide, 0.0)
-        total = jnp.sum(wide, axis=0, keepdims=True)
+        total = placed(flat, 96, WIDTH * i)[0:1]
         ib[:, WIDTH * i : WIDTH * (i + 1)] = jnp.broadcast_to(total, (8, WIDTH))
 
 
 class Scatter:
-    def __init__(self, at, s, r1, rd0, rd1, rx, ry, rz, cs, p2, p1, zs):
+    def __init__(self, at, s, r1, rd0, rd1, rx, ry, rz, early, cs, p2, p1, zs):
         self.at, self.s = at, s
+        self.early = early
         self.r1, self.rd0, self.rd1, self.rx, self.ry, self.rz = r1, rd0, rd1, rx, ry, rz
         self.cs, self.p2, self.p1, self.zs = cs, p2, p1, zs
 
@@ -243,27 +295,30 @@
         at = self.at
         return remote(self.s.at[ch, :, :, at.oc], self.r1.at[ch], self.cs, (ch,), at.to_c)
 
-    def p2_copies(self, ch):
-        at = self.at
+    def zs_of(self, ch, k):
+        return slice(None) if k is None else pl.ds(self.at.above(k), 1)
+
+    def p2_copies(self, ch, k=None):
+        at, some, index = self.at, self.zs_of(ch, k), k or 0
         head, tail = pl.ds(0, CUT), pl.ds(CUT, ROWS - CUT)
+        corner = self.s.at[ch, some, at.ox, at.c, at.oy]
         return (
-            remote(self.s.at[ch, :, at.ox, at.c, at.oy, head], self.rd0.at[ch], self.p2, (ch, 0), at.to_x),
-            remote(self.s.at[ch, :, at.ox, at.c, at.oy, tail], self.rd1.at[ch], self.p2, (ch, 1), at.to_y),
+            remote(corner.at[:, head], self.rd0.at[ch, some], self.p2, (ch, index, 0), at.to_x),
+            remote(corner.at[:, tail], self.rd1.at[ch, some], self.p2, (ch, index, 1), at.to_y),
         )
 
-    def p1_copies(self, ch):
-        at = self.at
+    def p1_copies(self, ch, k=None):
+        at, some, index = self.at, self.zs_of(ch, k), k or 0
         return (
-            remote(self.s.at[ch, :, at.ox, at.c, at.y], self.rx.at[ch], self.p1, (ch, 0), at.to_x),
-            remote(self.s.at[ch, :, at.x, at.c, at.oy], self.ry.at[ch], self.p1, (ch, 1), at.to_y),
+            remote(self.s.at[ch, some, at.ox, at.c, at.y], self.rx.at[ch, some], self.p1, (ch, index, 0), at.to_x),
+            remote(self.s.at[ch, some, at.x, at.c, at.oy], self.ry.at[ch, some], self.p1, (ch, index, 1), at.to_y),
         )
 
-    def z_copies(self, ch):
-        at = self.at
-        return [
-            remote(self.s.at[ch, at.above(k), at.x, at.c, at.y], self.rz.at[ch, k - 1], self.zs, (ch, k - 1), at.to_z(k))
-            for k in range(1, NZ)
-        ]
+    def z_copy(self, ch, k):
+        at = self.at
+        return remote(
+            self.s.at[ch, at.above(k), at.x, at.c, at.y], self.rz.at[ch, k - 1], self.zs, (ch, k - 1), at.to_z(k)
+        )
 
     def start(self, ch):
         self.c_copy(ch).start()
@@ -279,16 +334,23 @@
         at = self.at
         self.c_copy(ch).wait_recv()
         self.add_core(ch, at.ox, at.oy)
-        for copy in self.p2_copies(ch):
-            copy.start()
+        for k in (1, 2, 3, 0) if ch in FINE else (None,):
+            for copy in self.p2_copies(ch, k):
+                copy.start()
         self.add_core(ch, at.ox, at.y)
         self.add_core(ch, at.x, at.oy)
         self.add_core(ch, at.x, at.y)
 
-    def diagonal(self, ch):
-        at = self.at
-        over_x, over_y = self.p2_copies(ch)
-        to_x, to_y = self.p1_copies(ch)
+    def over(self, k, work):
+        if k is None:
+            loop(NZ, work)
+        else:
+            work(self.at.above(k))
+
+    def diagonal(self, ch, k=None):
+        at = self.at
+        over_x, over_y = self.p2_copies(ch, k)
+        to_x, to_y = self.p1_copies(ch, k)
         head, tail = pl.ds(0, CUT), pl.ds(CUT, ROWS - CUT)
         over_x.wait_recv()
 
@@ -296,7 +358,7 @@
             total = self.s[ch, z, at.x, at.c, at.oy, head].astype(F32) + self.rd0[ch, z].astype(F32)
             self.s[ch, z, at.x, at.c, at.oy, head] = total.astype(BF)
 
-        loop(NZ, first)
+        self.over(k, first)
         to_y.start()
         over_y.wait_recv()
 
@@ -304,12 +366,12 @@
             total = self.s[ch, z, at.ox, at.c, at.y, tail].astype(F32) + self.rd1[ch, z].astype(F32)
             self.s[ch, z, at.ox, at.c, at.y, tail] = total.astype(BF)
 
-        loop(NZ, second)
+        self.over(k, second)
         to_x.start()
 
-    def plane(self, ch):
-        at = self.at
-        for copy in self.p1_copies(ch):
+    def plane(self, ch, k=None):
+        at = self.at
+        for copy in self.p1_copies(ch, k):
             copy.wait_recv()
 
         def one(z):
@@ -317,21 +379,102 @@
             total = total + self.ry[ch, z].astype(F32)
             self.s[ch, z, at.x, at.c, at.y] = total.astype(BF)
 
-        loop(NZ, one)
-        for copy in self.z_copies(ch):
-            copy.start()
+        self.over(k, one)
+        for j in range(1, NZ) if k is None else (k,) if k else ():
+            self.z_copy(ch, j).start()
 
     def finish(self, ch):
         at = self.at
-        for copy in self.z_copies(ch):
-            copy.wait_recv()
+        for k in range(1, NZ):
+            self.z_copy(ch, k).wait_recv()
         total = self.s[ch, at.z, at.x, at.c, at.y].astype(F32)
         for k in range(NZ - 1):
             total = total + self.rz[ch, k].astype(F32)
         return total
 
     def drain(self, ch):
-        for copy in (self.c_copy(ch), *self.p2_copies(ch), *self.p1_copies(ch), *self.z_copies(ch)):
+        self.c_copy(ch).wait_send()
+        for k in range(NZ) if ch in FINE else (None,):
+            for copy in (*self.p2_copies(ch, k), *self.p1_copies(ch, k)):
+                copy.wait_send()
+        for k in range(1, NZ):
+            self.z_copy(ch, k).wait_send()
+
+
+    def early_z(self):
+        at = self.at
+        return [
+            remote(self.s.at[0, at.above(k), :, at.c], self.early.at[k - 1], self.zs, (0, k - 1), at.to_z(k))
+            for k in range(1, NZ)
+        ]
+
+    def early_p2(self):
+        at = self.at
+        head, tail = pl.ds(0, CUT), pl.ds(CUT, ROWS - CUT)
+        return (
+            remote(self.s.at[0, at.z, at.ox, at.c, at.oy, head], self.rd0.at[0, 0], self.p2, (0, 0, 0), at.to_x),
+            remote(self.s.at[0, at.z, at.ox, at.c, at.oy, tail], self.rd1.at[0, 0], self.p2, (0, 0, 1), at.to_y),
+        )
+
+    def early_p1(self):
+        at = self.at
+        return (
+            remote(self.s.at[0, at.z, at.ox, at.c, at.y], self.rx.at[0, 0], self.p1, (0, 0, 0), at.to_x),
+            remote(self.s.at[0, at.z, at.x, at.c, at.oy], self.ry.at[0, 0], self.p1, (0, 0, 1), at.to_y),
+        )
+
+    def early_core(self):
+        at = self.at
+        self.c_copy(0).wait_recv()
+
+        def one(i):
+            z, x, y = i // (NX * NY), rem(i // NY, NX), rem(i, NY)
+            total = self.s[0, z, x, at.c, y].astype(F32) + self.r1[0, z, x, y].astype(F32)
+            self.s[0, z, x, at.c, y] = total.astype(BF)
+
+        loop(NZ * NX * NY, one)
+        for copy in self.early_z():
+            copy.start()
+
+    def early_plane(self):
+        at = self.at
+        for copy in self.early_z():
+            copy.wait_recv()
+
+        def one(i):
+            x, y = i // NY, rem(i, NY)
+            total = self.s[0, at.z, x, at.c, y].astype(F32)
+            for k in range(NZ - 1):
+                total = total + self.early[k, x, y].astype(F32)
+            self.s[0, at.z, x, at.c, y] = total.astype(BF)
+
+        loop(NX * NY, one)
+        for copy in self.early_p2():
+            copy.start()
+
+    def early_diagonal(self):
+        at = self.at
+        over_x, over_y = self.early_p2()
+        to_x, to_y = self.early_p1()
+        head, tail = pl.ds(0, CUT), pl.ds(CUT, ROWS - CUT)
+        over_x.wait_recv()
+        total = self.s[0, at.z, at.x, at.c, at.oy, head].astype(F32) + self.rd0[0, 0].astype(F32)
+        self.s[0, at.z, at.x, at.c, at.oy, head] = total.astype(BF)
+        to_y.start()
+        over_y.wait_recv()
+        total = self.s[0, at.z, at.ox, at.c, at.y, tail].astype(F32) + self.rd1[0, 0].astype(F32)
+        self.s[0, at.z, at.ox, at.c, at.y, tail] = total.astype(BF)
+        to_x.start()
+
+    def early_finish(self):
+        at = self.at
+        for copy in self.early_p1():
+            copy.wait_recv()
+        total = self.s[0, at.z, at.x, at.c, at.y].astype(F32) + self.rx[0, 0].astype(F32)
+        return total + self.ry[0, 0].astype(F32)
+
+    def early_drain(self):
+        for copy in (self.c_copy(0), *self.early_z(), *self.early_p2(), *self.early_p1()):
             copy.wait_send()
 
 
@@ -429,29 +572,52 @@
 
 def gather_vectors(vg, ibg, sv):
     owners = GROUP * NY
-
-    def pieces(values, pick):
-        high = values.astype(BF)
-        rest = (values - high.astype(F32)).astype(BF)
+    across = lax.broadcasted_iota(jnp.int32, (WIDTH, 128), 0)
+    lane = lax.broadcasted_iota(jnp.int32, (WIDTH, 128), 1)
+
+    def pieces(wide, size, start):
+        pick = ((rem(across + start, size) == lane) & (lane < size)).astype(F32).astype(BF)
+        high = wide.astype(BF)
+        rest = (wide - high.astype(F32)).astype(BF)
         return product(high, pick) + product(rest, pick)
 
-    def grids(shape):
-        return [lax.broadcasted_iota(jnp.int32, shape, i) for i in range(len(shape))]
-
-    across, lane = grids((WIDTH, 128))
-    device, row, col = grids((owners, 16, WIDTH))
-    pick = ((rem(across, 24) == lane) & (lane < 24)).astype(F32).astype(BF)
-    first = device * 24
-    wide = jnp.where((col >= first) & (col < first + 24), vg[...][None], 0.0)
-    total = pieces(wide.reshape(owners * 16, WIDTH), pick)
-    first = device * 96
+    def owned(shape, size, start):
+        first = lax.broadcasted_iota(jnp.int32, shape, 0) * size - start
+        col = lax.broadcasted_iota(jnp.int32, shape, len(shape) - 1)
+        return (col >= first) & (col < first + size)
+
+    wide = jnp.where(owned((owners, 8, WIDTH), 24, 0), vg[...][None], 0.0)
+    total = pieces(wide.reshape(owners * 8, WIDTH), 24, 0)
+    sv[:, :, :, :, 0:8] = total.reshape(NZ, NX, NC, NY, 8, 128)
+    total = jnp.zeros((owners, 128), F32)
     for i in range(4):
-        pick = ((rem(across + WIDTH * i, 96) == lane) & (lane < 96)).astype(F32).astype(BF)
-        at = col + WIDTH * i
-        values = ibg[0:1, WIDTH * i : WIDTH * (i + 1)][None]
-        wide = jnp.where((at >= first) & (at < first + 96) & (row == 8), values, 0.0)
-        total = total + pieces(wide.reshape(owners * 16, WIDTH), pick)
-    sv[...] = total.reshape(sv.shape)
+        part = ibg[0:1, WIDTH * i : WIDTH * (i + 1)]
+        wide = jnp.where(owned((owners, WIDTH), 96, WIDTH * i), part, 0.0)
+        total = total + pieces(wide, 96, WIDTH * i)
+    total = jnp.broadcast_to(total[:, None, :], (owners, 8, 128))
+    sv[:, :, :, :, 8:16] = total.reshape(NZ, NX, NC, NY, 8, 128)
+
+
+def play(schedule, steps, loops):
+    at = 0
+    while at < len(schedule):
+        name, *numbers = schedule[at].split()
+        numbers = [int(n) for n in numbers]
+        if name not in loops:
+            steps[name](*numbers)
+            at += 1
+            continue
+        turns = [i for i, entry in enumerate(schedule) if entry.split()[0] == name]
+        between = [schedule[i + 1 : j] for i, j in zip(turns, turns[1:])]
+
+        def turn(i):
+            loops[name](i)
+            for index, entries in enumerate(between):
+                if entries:
+                    pl.when(i == index)(partial(play, entries, steps, {}))
+
+        loop(len(turns), turn)
+        at = turns[-1] + 1
 
 
 QB, VB, OB, G1, S1, UB, G2, S2 = range(8)
@@ -463,20 +629,21 @@
     out, igrad, dq, dk, dv, do, di, du, dsmall, saved,
     g, gv, wd, u, page, cot, dead, hid, qkv, outp, xt, hidt, ctxt,
     n1, inv1, acc1, acc2, dst, bias, vec, ib, vg, ibg,
-    sv, r1, rd0, rd1, rx, ry, rz, vc, vx, vy, vz,
+    sv, r1, rd0, rd1, rx, ry, rz, early, vc, vx, vy, vz,
     zs, zr, p1s, p1r, p2s, p2r, cs, cr, vs, vr, es, er,
     css, csr, q2s, q2r, q1s, q1r, zss, zsr, ws, wr, loads, saves,
 ):
     at = Place(stride)
     gather = Gather(at, g, (zs, zr), (p1s, p1r), (p2s, p2r), (cs, cr))
     scatter = Scatter(
-        at, g, r1, rd0, rd1, rx, ry, rz, (css, csr), (q2s, q2r), (q1s, q1r), (zss, zsr)
+        at, g, r1, rd0, rd1, rx, ry, rz, early, (css, csr), (q2s, q2r), (q1s, q1r), (zss, zsr)
     )
     vector = VectorScatter(at, sv, vc, vx, vy, vz, (ws, wr))
 
     def put(ch, value):
         g[ch, at.z, at.x, at.c, at.y] = value
 
+    at.hail()
     pack_weights((q, k, v, o, inner, outer), put)
     gv[at.z, at.x, at.c, at.y] = small[...]
     own = pl.ds(pl.multiple_of(at.y * 256, 256), 256)
@@ -487,67 +654,60 @@
     ]
     for copy in local:
         copy.start()
-    at.greet()
+    at.meet()
 
     ve, ee = (vs, vr), (es, er)
-    swaps = [
-        remote(hidden.at[at.oy], page.at[own], ee, 0, at.to_y),
-        remote(mask.at[at.oy], dead.at[at.y], ee, 1, at.to_y),
-        remote(grad.at[at.oy], cot.at[own], ee, 2, at.to_y),
-        remote(outp.at[theirs], out.at[at.y], ee, 3, at.to_y),
-        remote(cot.at[theirs], igrad.at[at.y], ee, 4, at.to_y),
-    ]
+    page_in = remote(hidden.at[at.oy], page.at[own], ee, 0, at.to_y)
+    mask_in = remote(mask.at[at.oy], dead.at[at.y], ee, 1, at.to_y)
+    grad_in = remote(grad.at[at.oy], cot.at[own], ee, 2, at.to_y)
+    out_over = remote(outp.at[theirs], out.at[at.y], ee, 3, at.to_y)
+    grad_over = remote(cot.at[theirs], igrad.at[at.y], ee, 4, at.to_y)
+    swaps = [page_in, mask_in, grad_in, out_over, grad_over]
     mine = gv.at[at.z, at.x, at.c, at.y]
+    line = gv.at[:, at.x, at.c, at.y]
+    pairs = gv.at[:, :, at.c, at.y]
+    core = gv.at[:, :, at.c]
     vzs = [remote(mine, mine, ve, kk - 1, at.to_z(kk)) for kk in range(1, NZ)]
-    for copy in vzs:
-        copy.start()
-    swaps[0].start()
-    swaps[1].start()
-    gather.start_z(0)
-    gather.start_own(0)
-    gather.start_z(1)
-    gather.start_own(1)
-    for copy in vzs:
-        copy.wait_recv()
-    line = gv.at[:, at.x, at.c, at.y]
     vxs = remote(line, line, ve, 3, at.to_x)
-    vxs.start()
-    loop(CHUNKS - 2, lambda i: gather.start_z(i + 2))
-    dead[at.y] = mask[at.y]
-    vxs.wait_recv()
-    pairs = gv.at[:, :, at.c, at.y]
     vys = remote(pairs, pairs, ve, 4, at.to_y)
-    vys.start()
-    gather.plane(0)
-    vys.wait_recv()
-    core = gv.at[:, :, at.c]
     vcs = remote(core, core, ve, 5, at.to_c)
-    vcs.start()
-
-    gather.start_own(2)
-    gather.plane(1)
-    gather.diagonal(0)
-    vcs.wait_recv()
-    spread(gv, vec, ib)
-    gather.start_own(3)
-    gather.plane(2)
-    gather.diagonal(1)
-    gather.cross(0)
-    for copy in local:
-        copy.wait()
-    swaps[0].wait_recv()
-    swaps[1].wait_recv()
+
+    def vector_z():
+        for copy in vzs:
+            copy.start()
+
+    def vector_x():
+        for copy in vzs:
+            copy.wait_recv()
+        vxs.start()
+
+    def vector_y():
+        vxs.wait_recv()
+        vys.start()
+
+    def vector_c():
+        vys.wait_recv()
+        vcs.start()
+
+    def page_start():
+        page_in.start()
+        mask_in.start()
+
+    def page_wait():
+        for copy in local:
+            copy.wait()
+        page_in.wait_recv()
+        mask_in.wait_recv()
 
     def turn(i):
         xt[tile(i, 256), :] = page[:, tile(i, 256)].T
 
-    loop(3, turn)
-    for half in range(2):
-        bias[256 * half : 256 * half + 256] = jnp.broadcast_to(dead[half, 0:1].T, (256, 128))
-    gather.start_own(4)
-    gather.plane(3)
-    gather.arrive(0)
-    unpack_weights(g, 0, wd)
+    def prepare():
+        dead[at.y] = mask[at.y]
+        loop(3, turn)
+        for half in range(2):
+            bias[256 * half : 256 * half + 256] = jnp.broadcast_to(dead[half, 0:1].T, (256, 128))
+        spread(gv, vec, ib)
 
     def queries(i):
         cols = tile(i, 256)
@@ -563,15 +723,10 @@
         value = product(page[...], wd[:, cols]) + vec[VB : VB + 1, tile(i, 256)]
         qkv[:, cols] = value.astype(BF)
 
-    loop(3, queries)
-    loop(3, keys)
-    gather.diagonal(2)
-    gather.cross(1)
-    gather.start_own(5)
-    gather.plane(4)
-    gather.arrive(1)
-    unpack_weights(g, 1, wd)
-    loop(3, vals)
+    def queries_keys():
+        loop(3, queries)
+        loop(3, keys)
+
     lane = lax.broadcasted_iota(jnp.int32, (512, 128), 1)
     sides = (lane < 64, lane >= 64)
 
@@ -601,45 +756,10 @@
         outp[:, tile(pair, 128)] = total.T.astype(BF)
         save(pair).start()
 
-    def steps(*table):
-        def run(i):
-            for index, work in enumerate(table):
-                pl.when(i == index)(work)
-
-        return run
-
-    def attend_and(table):
-        def run(i):
-            attend(i)
-            steps(*table)(i)
-
-        return run
-
-    def start_cot():
-        swaps[2].start()
-        gather.cross(2)
-
-    loop(
-        6,
-        attend_and(
-            (
-                lambda: gather.diagonal(3),
-                start_cot,
-                lambda: gather.plane(5),
-                lambda: gather.diagonal(4),
-                lambda: gather.cross(3),
-            )
-        ),
-    )
-
     def attended(i):
         cols = tile(i, 256)
         value = product(outp[...], wd[:, tile(i + 9, 256)]) + vec[OB : OB + 1, cols]
         acc1[:, cols] = page[:, cols].astype(F32) + value
-
-    loop(3, attended)
-    gather.diagonal(5)
-    gather.cross(4)
 
     def first_norm(i):
         rows = tile(i, 64)
@@ -651,18 +771,14 @@
         inv1[rows, :] = jnp.broadcast_to(inverse, (64, 128))
         hid[rows, :] = (normed * vec[G1 : G1 + 1] + vec[S1 : S1 + 1]).astype(BF)
 
-    loop(8, first_norm)
-
     def turn_hidden(i):
         hidt[tile(i, 256), :] = hid[:, tile(i, 256)].T
 
-    loop(3, turn_hidden)
-    gather.arrive(2)
-    unpack_weights(g, 2, wd)
-    gather.arrive(3)
-    unpack_weights(g, 3, wd)
-    loop(6, lambda i: save(i).wait())
-    gather.cross(5)
+    def after_attention():
+        loop(3, attended)
+        loop(8, first_norm)
+        loop(3, turn_hidden)
+        loop(6, lambda i: save(i).wait())
 
     def feed(i):
         cols = tile(i, 384)
@@ -679,15 +795,10 @@
 
         loop(8, one)
 
-    loop(8, feed)
-    for half in range(2):
-        gather.arrive(4 + half)
+    def outer_half(half):
         cols = slice(COLS * half, COLS * half + COLS)
         weight = g[4 + half].reshape(8 * COLS, COLS)
         acc1[:, cols] = product(u[:, 0:3072], weight)
-    swaps[2].wait_recv()
-
-    vg[...] = jnp.zeros_like(vg)
 
     def second_norm(i):
         rows = tile(i, 64)
@@ -707,30 +818,59 @@
         page[rows, :] = low
         vg[UB : UB + 1] += column(low.astype(F32))
 
+    play(
+        FORWARD,
+        {
+            "z": gather.start_z,
+            "own": gather.start_own,
+            "plane": gather.plane,
+            "turn": gather.turn,
+            "cross": gather.cross,
+            "arrive": gather.arrive,
+            "late_z": gather.late_z,
+            "late_cross": gather.late_cross,
+            "vector_z": vector_z,
+            "vector_x": vector_x,
+            "vector_y": vector_y,
+            "vector_c": vector_c,
+            "vector_wait": vcs.wait_recv,
+            "page": page_start,
+            "page_wait": page_wait,
+            "grad": grad_in.start,
+            "grad_wait": grad_in.wait_recv,
+            "prepare": prepare,
+            "unpack": lambda ch: unpack_weights(g, ch, wd),
+            "queries_keys": queries_keys,
+            "values": lambda: loop(3, vals),
+            "after_attention": after_attention,
+            "outer": outer_half,
+        },
+        {"attend": attend, "feed": feed, "feed_on": lambda i: feed(i + 4)},
+    )
+    vg[...] = jnp.zeros_like(vg)
     loop(8, second_norm)
-    swaps[3].start()
+
+    low = page
     keep = pltpu.make_async_copy(outp.at[own], out.at[at.y], loads.at[0])
-    keep.start()
-
-    low = page
-    loop(CHUNKS, gather.drain)
-
-    def outer_grad(i):
-        z, x = i // 2, rem(i, 2)
-        value = product_left(u[:, tile(i, 384)], low[...]).astype(BF)
-        for half in range(2):
-            part = value[:, COLS * half : COLS * half + COLS]
-            g[half, z, x] = part.reshape(NC, NY, ROWS, COLS)
-
-    loop(8, outer_grad)
-    scatter.start(0)
-    scatter.start(1)
+    loop(CHUNKS - 1, gather.drain)
+    gather.late_drain()
+
+    def out_start():
+        out_over.start()
+        keep.start()
+
+    def outer_grad(half, slot):
+        def one(i):
+            z, x = i // 2, rem(i, 2)
+            cols = slice(COLS * half, COLS * half + COLS)
+            value = product_left(u[:, tile(i, 384)], low[:, cols]).astype(BF)
+            g[slot, z, x] = value.reshape(NC, NY, ROWS, COLS)
+
+        loop(8, one)
 
     def load(part):
         cols = pl.ds(3072 * part, 3072)
         return pltpu.make_async_copy(saved.at[:, cols], u.at[:, cols], loads.at[1])
-
-    load(0).start()
 
     def inner_back(i):
         z, x = i // 2, rem(i, 2)
@@ -742,9 +882,6 @@
         total = column(value.astype(F32))
         ibg[:, tile(i, 384)] = jnp.broadcast_to(total, (8, 384))
 
-    loop(8, inner_back)
-    scatter.core(0)
-
     def weight_grad(slot, unit, left, right):
         def one(i):
             value = product(left[tile(i, 384), :], right)
@@ -760,24 +897,9 @@
         right = u[:, 3072 + WIDTH * unit : 3072 + WIDTH * (unit + 1)]
         weight_grad(2 + unit // 2, unit % 2, hidt, right)
 
-    inner_grad(0)
-    inner_grad(1)
-    scatter.start(2)
-    scatter.core(1)
-    inner_grad(2)
-    inner_grad(3)
-    scatter.start(3)
-    scatter.diagonal(0)
-
     def hidden_back(i):
         cols = tile(i, 256)
         acc2[:, cols] = acc2[:, cols] + product_right(u[:, 3072:6144], wd[cols, 4 * WIDTH :])
-
-    loop(3, hidden_back)
-    load(0).wait()
-    load(1).start()
-    scatter.core(2)
-    scatter.diagonal(1)
 
     def first_back(i):
         rows = tile(i, 64)
@@ -793,16 +915,9 @@
         low[rows, :] = short
         vg[OB : OB + 1] += column(short.astype(F32))
 
-    loop(8, first_back)
-    weight_grad(4, 1, ctxt, low[...])
-
     def context_back(i):
         cols = tile(i, 256)
         hid[:, cols] = product_right(low[...], wd[cols, 3 * WIDTH : 4 * WIDTH]).astype(BF)
-
-    loop(3, context_back)
-    scatter.plane(0)
-    load(1).wait()
 
     def attend_back(pair):
         at_q, at_k, at_v = tile(pair, 128), tile(pair + 6, 128), tile(pair + 12, 128)
@@ -826,66 +941,27 @@
         qkv[:, at_k] = dk2.astype(BF)
         qkv[:, at_v] = dv2.astype(BF)
 
-    def back_and(table):
-        def run(i):
-            attend_back(i)
-            steps(*table)(i)
-
-        return run
-
-    loop(
-        6,
-        back_and(
-            (
-                lambda: scatter.diagonal(2),
-                lambda: scatter.core(3),
-                lambda: scatter.plane(1),
-                lambda: scatter.diagonal(3),
-                lambda: scatter.plane(2),
-            )
-        ),
-    )
-    weight_grad(4, 0, xt, qkv[:, 2 * WIDTH : 3 * WIDTH])
-    scatter.start(4)
-    weight_grad(5, 0, xt, qkv[:, 0:WIDTH])
-    scatter.core(4)
-    weight_grad(5, 1, xt, qkv[:, WIDTH : 2 * WIDTH])
-    scatter.start(5)
-
     def sums(i):
         rows = tile(i, 64)
         vg[QB : QB + 1] += column(qkv[rows, 0:WIDTH].astype(F32))
         vg[VB : VB + 1] += column(qkv[rows, 2 * WIDTH : 3 * WIDTH].astype(F32))
 
-    loop(8, sums)
-    gather_vectors(vg, ibg, sv)
-    vector.start()
-    scatter.diagonal(4)
-    scatter.core(5)
-    scatter.plane(3)
-    vector.core()
-
     def input_back(i):
         cols = tile(i, 256)
         value = acc2[:, cols] + product_right(qkv[...], wd[cols, 0 : 3 * WIDTH])
         cot[:, cols] = value.astype(BF)
 
-    loop(3, input_back)
-    vector.over_x()
-    scatter.diagonal(5)
-    swaps[4].start()
     keep_in = pltpu.make_async_copy(cot.at[own], igrad.at[at.y], loads.at[1])
-    keep_in.start()
-    scatter.plane(4)
-    vector.over_y()
-
-    outs = (q, k, v, o)
-    targets = (dq, dk, dv, do)
+
+    def grad_start():
+        grad_over.start()
+        keep_in.start()
 
     def finish(n):
-        total = scatter.finish(n)
+        total = scatter.finish(n) if n else scatter.early_finish()
         if n < 2:
-            du[:, COLS * n : COLS * n + COLS] = total
+            half = 1 - n
+            du[:, COLS * half : COLS * half + COLS] = total
         elif n < 4:
             for unit in range(2):
                 index = 2 * (n - 2) + unit
@@ -895,18 +971,69 @@
             first[...] = unfold(total, 0)
             second[...] = unfold(total, 1)
 
-    for n in range(4):
-        finish(n)
-    scatter.plane(5)
-    dsmall[...] = vector.finish()
-    finish(4)
-    finish(5)
-
+    def vector_finish():
+        dsmall[...] = vector.finish()
+
+    def context_grad():
+        load(1).start()
+        loop(3, context_back)
+        load(1).wait()
+
+    def outer_second():
+        outer_grad(1, 0)
+        load(0).start()
+
+    def output_grad():
+        weight_grad(4, 1, ctxt, low[...])
+
+    def first_grad():
+        loop(8, first_back)
+        load(0).wait()
+
+    play(
+        BACKWARD,
+        {
+            "start": scatter.start,
+            "core": scatter.core,
+            "diagonal": scatter.diagonal,
+            "plane": scatter.plane,
+            "finish": finish,
+            "early_core": scatter.early_core,
+            "early_plane": scatter.early_plane,
+            "early_diagonal": scatter.early_diagonal,
+            "vector": vector.start,
+            "vector_core": vector.core,
+            "vector_x": vector.over_x,
+            "vector_y": vector.over_y,
+            "vector_finish": vector_finish,
+            "out": out_start,
+            "grad": grad_start,
+            "outer_first": lambda: outer_grad(0, 1),
+            "outer_second": outer_second,
+            "inner_grad": inner_grad,
+            "first_back": first_grad,
+            "output_grad": output_grad,
+            "context_back": context_grad,
+            "value_grad": lambda: weight_grad(4, 0, xt, qkv[:, 2 * WIDTH : 3 * WIDTH]),
+            "query_grad": lambda: weight_grad(5, 0, xt, qkv[:, 0:WIDTH]),
+            "key_grad": lambda: weight_grad(5, 1, xt, qkv[:, WIDTH : 2 * WIDTH]),
+            "sums": lambda: loop(8, sums),
+            "gather_vectors": lambda: gather_vectors(vg, ibg, sv),
+        },
+        {
+            "inner_back": inner_back,
+            "hidden_back": hidden_back,
+            "attend_back": attend_back,
+            "input_back": input_back,
+        },
+    )
     keep.wait()
     keep_in.wait()
-    swaps[3].wait_recv()
-    swaps[4].wait_recv()
-    loop(CHUNKS, scatter.drain)
+    out_over.wait_recv()
+    grad_over.wait_recv()
+    for n in range(1, CHUNKS):
+        scatter.drain(n)
+    scatter.early_drain()
     vector.drain()
     for copy in vzs + [vxs, vys, vcs] + swaps:
         copy.wait_send()
@@ -957,9 +1084,9 @@
             full(512, WIDTH),
             low(512, 512),
             full(512, 128),
-            full(16, WIDTH),
+            full(8, WIDTH),
             full(8, 4 * WIDTH),
-            full(16, WIDTH),
+            full(8, WIDTH),
             full(8, 4 * WIDTH),
             full(NZ, NX, NC, NY, 16, 128),
             low(CHUNKS, NZ, NX, NY, ROWS, COLS),
@@ -968,6 +1095,7 @@
             low(CHUNKS, NZ, ROWS, COLS),
             low(CHUNKS, NZ, ROWS, COLS),
             low(CHUNKS, NZ - 1, ROWS, COLS),
+            low(NZ - 1, NX, NY, ROWS, COLS),
             full(NZ, NX, NY, 16, 128),
             full(NZ, NY, 16, 128),
             full(NZ, 16, 128),
@@ -979,8 +1107,8 @@
             *pair(6),
             *pair(5),
             *pair(CHUNKS),
-            *pair(CHUNKS, 2),
-            *pair(CHUNKS, 2),
+            *pair(CHUNKS, NZ, 2),
+            *pair(CHUNKS, NZ, 2),
             *pair(CHUNKS, NZ - 1),
             *pair(6),
             dma((2,)),
@@ -991,6 +1119,37 @@
         ),
         name="layer",
     )(*args)
+
+
+def hand_out_kernel(*refs):
+    large, small, outs, vectors = refs[:8], refs[8], refs[9:17], refs[17:26]
+    held, into, back = refs[26:34], refs[34], refs[35]
+    loads = [pltpu.make_async_copy(a, b, into.at[i]) for i, (a, b) in enumerate(zip(large, held))]
+    stores = [pltpu.make_async_copy(a, b, back.at[i]) for i, (a, b) in enumerate(zip(held, outs))]
+    for copy in loads:
+        copy.start()
+    for i, ref in enumerate(vectors):
+        ref[...] = small[i, : ref.shape[0]]
+    for load, store in zip(loads, stores):
+        load.wait()
+        store.start()
+    for store in stores:
+        store.wait()
+
+
+def hand_out(large, small):
+    vmem = pl.BlockSpec(memory_space=pltpu.VMEM)
+    hbm = pl.BlockSpec(memory_space=pl.ANY)
+    vectors = [jax.ShapeDtypeStruct((24,), F32)] * 8 + [jax.ShapeDtypeStruct((96,), F32)]
+    return pl.pallas_call(
+        hand_out_kernel,
+        out_shape=tuple([jax.ShapeDtypeStruct(v.shape, v.dtype) for v in large] + vectors),
+        in_specs=[hbm] * 8 + [vmem],
+        out_specs=tuple([hbm] * 8 + [vmem] * 9),
+        scratch_shapes=[pltpu.VMEM(v.shape, v.dtype) for v in large]
+        + [pltpu.SemaphoreType.DMA((8,)), pltpu.SemaphoreType.DMA((8,))],
+        name="hand_out",
+    )(*large, small)
 
 
 def body(
@@ -1036,28 +1195,11 @@
     weights = [
         coarse(v) for v in (query_weight, key_weight, value_weight, output_weight, inner_weight, outer_weight)
     ]
-    output, input_grad, dq, dk, dv, do, di, du, dsmall, _ = layer_call(
-        stride, (*weights, small, hidden_in, out_grad, mask)
-    )
-    qbg, vbg, obg, g1g, s1g, ubg, g2g, s2g = [fine(dsmall[i, :24]) for i in range(8)]
+    *large, dsmall, _ = layer_call(stride, (*weights, small, hidden_in, out_grad, mask))
+    output, input_grad, *grads = hand_out(large, dsmall)
+    dq, dk, dv, do, di, du, qbg, vbg, obg, g1g, s1g, ubg, g2g, s2g, ibg = [fine(v) for v in grads]
     return (
-        output,
-        input_grad,
-        fine(dq),
-        qbg,
-        fine(dk),
-        fine(dv),
-        vbg,
-        fine(do),
-        obg,
-        g1g,
-        s1g,
-        fine(di),
-        fine(dsmall[8, :96]),
-        fine(du),
-        ubg,
-        g2g,
-        s2g,
+        output, input_grad, dq, qbg, dk, dv, vbg, do, obg, g1g, s1g, di, ibg, du, ubg, g2g, s2g,
     )
 
 

time: 209 us -> 174 us (0.83)
  Pallas kernels: 188 us -> 170 us
  local copies, waits for them, and re-layouts: 17.7 us -> 1.4 us
    pallas_call x1, Pallas kernels: 188 us -> 166 us  [layer_call(): pl.pallas_call(partial(layer_kernel, stride), out_shape=tuple(tokens + gr...]
    unnamed x8 -> x0, local copies, waits for them, and re-layouts: 13.6 us -> none
    pallas_call x0 -> x1, Pallas kernels: none -> 3.96 us  [hand_out(): pl.pallas_call(hand_out_kernel, out_shape=tuple([jax.ShapeDtypeStruct(v.s...]
    squeeze x2 -> x0, local copies, waits for them, and re-layouts: 2.69 us -> none  [the longest x1 1.51 us: body(): dsmall[i, :24]]
where the time goes in v1:
time: 174 us
  Pallas kernels  170 us (98%)
  other arithmetic  2.01 us (1%)
    pallas_call x1, Pallas kernels, layer_call(): pl.pallas_call(partial(layer_kernel, stride), out_shape=tuple(tokens + gr...  166 us
    pallas_call x1, Pallas kernels, hand_out(): pl.pallas_call(hand_out_kernel, out_shape=tuple([jax.ShapeDtypeStruct(v.s...  3.96 us

profile of v1, /device:TPU:0, one launch (start us, length us, event | category | flops | bytes accessed | tf_op | source)
XLA Modules:
  0.0 173.8 jit_solution(2134193882732010944)
XLA Ops:
  0.7 0.8 and_select_fusion
  1.4 0.8 stack.35
  2.2 1.3 fusion.2.small
  3.5 0.6 broadcast_in_dim.22.mask
  4.1 165.6 %layer.1 = (bf16[2,256,768]{2,1,0:T(8,128)(2,1)}, bf16[2,256,768]{2,1,0:T(8,128)(2,1)}, f32[24,768]{1,0:T(8,128)}, f32[24,768]{1,0:T(8,128)}, f32[24,768]{1,0:T(...) custom-call(bf16[24,768]{1,0:T(8,128)(2,1)} %q.1, ...), custom_call_target="tpu_custom_call" | custom-call | tf_op jit(solution)/shard_map/layer/pallas_call | solution.py:1062
  169.6 4.0 %hand_out.1 = (bf16[2,256,768]{2,1,0:T(8,128)(2,1)}, bf16[2,256,768]{2,1,0:T(8,128)(2,1)}, f32[24,768]{1,0:T(8,128)}, f32[24,768]{1,0:T(8,128)}, f32[24,768]{1,0...) custom-call(bf16[2,256,768]{2,1,0:T(8,128)(2,1)} %get-tuple-element., ...), custom_call_target="tpu_custom_call" | custom-call | tf_op jit(solution)/shard_map/hand_out/pallas_call | solution.py:1144
  (1 shorter events, 0.0 us)

commit v2 on v1

--- a/solution.py
+++ b/solution.py
@@ -16,38 +16,40 @@
 CHUNKS = 6
 ROWS, COLS = 96, 384
 LATE = 5
+FINE_G, COARSE = (0, 1), (2, 3, 4)
+G_STEPS = NZ * len(FINE_G) + len(COARSE) + 1
 CUT = 64
 WIDTH = 768
 FINE = (4, 5)
+S_STEPS = FINE[0] + NZ * len(FINE)
 BF, F32 = jnp.bfloat16, jnp.float32
-VMEM_LIMIT = 62 * 2**20
+VMEM_LIMIT = 63 * 2**20
 
 FORWARD = (
-    "own 1", "own 5", "vector_z", "z 0", "turn 1 0", "page", "own 2", "vector_x", "own 0", "turn 5 0",
-    "plane 0 3", "z 1", "plane 0 1", "page_wait", "z 2", "plane 1 3", "z 4", "plane 1 1", "plane 1 2",
-    "turn 0 3", "plane 0 2", "vector_y", "turn 0 1", "turn 0 0", "turn 1 3", "turn 1 2", "z 3", "turn 0 2",
-    "turn 1 1", "plane 4 2", "plane 2 3", "late_z", "cross 0", "vector_c", "plane 2 1", "own 3", "plane 2 2",
-    "cross 1", "vector_wait", "arrive 0", "plane 3 1", "prepare", "unpack 0", "plane 3 3", "own 4", "turn 2 3",
-    "turn 2 1", "arrive 1", "unpack 1", "queries_keys", "turn 2 2", "plane 3 2", "turn 2 0", "values",
-    "turn 3 1", "attend 0", "attend 1", "plane 4 3", "attend 2", "attend 3", "turn 3 0", "plane 4 1", "cross 2",
-    "turn 3 3", "attend 4", "turn 3 2", "grad", "turn 4 0", "attend 5", "arrive 2", "after_attention",
-    "unpack 2", "cross 3", "feed 0", "turn 4 3", "feed 1", "turn 4 2", "feed 2", "late_cross", "arrive 3",
-    "turn 4 1", "feed 3", "unpack 3", "feed_on 4", "cross 4", "feed_on 5", "feed_on 6", "feed_on 7", "arrive 4",
-    "arrive 5", "outer 0", "grad_wait", "outer 1",
+    "vector_z", "own 1", "z 0", "own 5", "page", "z 1", "turn 1 0", "own 0", "z 2", "plane 0 2", "vector_x",
+    "plane 0 1", "z 3", "turn 5 0", "plane 0 3", "plane 1 1", "plane 1 2", "plane 1 3", "turn 0 2", "vector_y",
+    "turn 0 1", "turn 0 0", "turn 0 3", "turn 1 1", "turn 1 2", "z 4", "turn 1 3", "plane_all 2", "vector_c",
+    "vector_wait", "page_wait", "late_z", "cross 0", "cross 1", "plane_all 3", "arrive 0", "prepare",
+    "arrive 1", "late_arrive 0", "unpack 1", "unpack 0", "queries_keys", "turn 2", "values", "attend 0",
+    "plane_all 4", "attend 1", "turn 3", "attend 2", "attend 3", "cross 2", "attend 4", "attend 5",
+    "after_attention", "arrive 2", "turn 4", "grad", "unpack 2", "feed 0", "late_cross 1", "feed 1", "cross 3",
+    "feed 2", "late_arrive 1", "feed 3", "arrive 3", "unpack 3", "late_cross 3", "late_cross 2", "feed_on 4",
+    "cross 4", "feed_on 5", "feed_on 6", "late_arrive 2", "feed_on 7", "arrive 4", "outer_left",
+    "outer_right 0", "grad_wait", "outer_right 1", "late_arrive 3", "cotangent", "outer_right 2",
+    "outer_right 3",
 )
 BACKWARD = (
-    "out", "outer_first", "start 1", "outer_second", "inner_back 0", "inner_back 1", "start 0", "core 1",
-    "inner_back 2", "inner_back 3", "inner_back 4", "early_core", "inner_back 5", "inner_back 6", "diagonal 1",
-    "inner_back 7", "inner_grad 0", "inner_grad 1", "start 2", "inner_grad 2", "inner_grad 3", "hidden_back 0",
-    "hidden_back 1", "core 2", "start 3", "hidden_back 2", "first_back", "context_back", "core 3",
-    "attend_back 0", "diagonal 2", "attend_back 1", "attend_back 2", "diagonal 3", "attend_back 3",
-    "attend_back 4", "output_grad", "attend_back 5", "query_grad", "plane 1", "value_grad", "start 4",
-    "key_grad", "early_plane", "sums", "start 5", "gather_vectors", "vector", "core 4", "plane 2",
-    "vector_core", "core 5", "plane 3", "diagonal 4 2", "diagonal 4 0", "finish 1", "input_back 0",
-    "diagonal 4 1", "vector_x", "diagonal 4 3", "vector_y", "diagonal 5 2", "diagonal 5 0", "plane 4 2",
-    "diagonal 5 1", "input_back 1", "early_diagonal", "finish 2", "plane 4 0", "diagonal 5 3", "plane 4 1",
-    "finish 3", "input_back 2", "vector_finish", "grad", "plane 5 2", "plane 5 1", "plane 4 3", "plane 5 3",
-    "finish 4", "plane 5 0", "finish 0", "finish 5",
+    "out", "outer_first", "start 1", "outer_second", "start 0", "inner_back 0", "core 1", "inner_back 1",
+    "early_core", "inner_back 2", "inner_back 3", "inner_grad 0", "diagonal 1", "inner_grad 1", "start 2",
+    "inner_grad 2", "inner_grad 3", "hidden_back 0", "start 3", "hidden_back 1", "hidden_back 2", "core 2",
+    "first_back", "output_grad", "core 3", "context_back", "diagonal 2", "attend_back 0", "plane 1",
+    "attend_back 1", "attend_back 2", "diagonal 3", "attend_back 3", "attend_back 4", "attend_back 5",
+    "value_grad", "start 4", "key_grad", "query_grad", "start 5", "sums", "plane 2", "core 4", "core 5",
+    "diagonal 4 2", "early_plane", "plane 3", "diagonal 4 0", "gather_vectors", "vector", "diagonal 4 3",
+    "diagonal 5 3", "vector_core", "diagonal 5 2", "early_diagonal", "finish 1", "input_back 0", "diagonal 4 1",
+    "plane 4 2", "diagonal 5 1", "diagonal 5 0", "finish 3", "plane 4 3", "plane 4 0", "plane 5 3",
+    "input_back 1", "vector_x", "input_back 2", "grad", "plane 5 2", "finish 2", "vector_y", "plane 4 1",
+    "finish 0", "plane 5 1", "vector_finish", "plane 5 0", "finish 4", "finish 5",
 )
 
 
@@ -102,12 +104,12 @@
         pl.semaphore_wait(pltpu.get_barrier_semaphore(), NZ + 2)
 
 
-def remote(src, dst, sems, index, who):
+def remote(src, dst, sems, index, who, group=None):
     send, recv = sems
     return pltpu.make_async_remote_copy(
         src_ref=src,
         dst_ref=dst,
-        send_sem=send.at[index],
+        send_sem=send.at[index if group is None else group],
         recv_sem=recv.at[index],
         device_id=who,
         device_id_type=pl.DeviceIdType.MESH,
@@ -131,22 +133,29 @@
         at = self.at
         z = at.z if mine else at.below(k)
         ref = self.g.at[ch, z, at.x, at.c, at.y]
-        return remote(ref, ref, self.zs, (ch, k - 1), at.to_z(k))
+        return remote(ref, ref, self.zs, (ch, k - 1), at.to_z(k), (ch,))
+
+    def some(self, ch, k):
+        if ch in COARSE:
+            return slice(None), NZ * len(FINE_G) + COARSE.index(ch)
+        if ch == LATE:
+            return pl.ds(self.at.z, 1), NZ * len(FINE_G) + len(COARSE)
+        return pl.ds(self.at.below(k), 1), NZ * FINE_G.index(ch) + k
 
     def p1_copies(self, ch, k, mine=True):
         at = self.at
-        z = at.below(k)
+        z, index = self.some(ch, k)
         x, y = (at.x, at.y) if mine else (at.ox, at.oy)
         over_x = self.g.at[ch, z, x, at.c, at.y]
         over_y = self.g.at[ch, z, at.x, at.c, y]
         return (
-            remote(over_x, over_x, self.p1, (ch, k, 0), at.to_x),
-            remote(over_y, over_y, self.p1, (ch, k, 1), at.to_y),
+            remote(over_x, over_x, self.p1, (index, 0), at.to_x, (ch,)),
+            remote(over_y, over_y, self.p1, (index, 1), at.to_y, (ch,)),
         )
 
     def p2_copies(self, ch, k, mine=True):
         at = self.at
-        z = at.below(k)
+        z, index = self.some(ch, k)
         head, tail = pl.ds(0, CUT), pl.ds(CUT, ROWS - CUT)
         if mine:
             over_x = self.g.at[ch, z, at.x, at.c, at.oy, head]
@@ -155,8 +164,8 @@
             over_x = self.g.at[ch, z, at.ox, at.c, at.oy, head]
             over_y = self.g.at[ch, z, at.ox, at.c, at.oy, tail]
         return (
-            remote(over_x, over_x, self.p2, (ch, k, 0), at.to_x),
-            remote(over_y, over_y, self.p2, (ch, k, 1), at.to_y),
+            remote(over_x, over_x, self.p2, (index, 0), at.to_x, (ch,)),
+            remote(over_y, over_y, self.p2, (index, 1), at.to_y, (ch,)),
         )
 
     def c_copy(self, ch, mine=True):
@@ -177,7 +186,13 @@
         for copy in self.p1_copies(ch, k):
             copy.start()
 
-    def turn(self, ch, k):
+    def plane_all(self, ch):
+        for k in range(1, NZ):
+            self.z_copy(ch, k, False).wait_recv()
+        for copy in self.p1_copies(ch, 0):
+            copy.start()
+
+    def turn(self, ch, k=0):
         from_x, from_y = self.p1_copies(ch, k, False)
         over_x, over_y = self.p2_copies(ch, k)
         from_y.wait_recv()
@@ -186,48 +201,57 @@
         over_y.start()
 
     def cross(self, ch):
-        def one(k):
+        for k in range(NZ) if ch in FINE_G else (0,):
             for copy in self.p2_copies(ch, k, False):
                 copy.wait_recv()
-
-        loop(NZ, one)
         self.c_copy(ch).start()
 
+    def arrive(self, ch):
+        self.c_copy(ch, False).wait_recv()
+
+
     def late_copy(self, k, mine=True):
         at = self.at
         ref = self.g.at[LATE, at.z if mine else at.below(k), :, at.c]
-        return remote(ref, ref, self.zs, (LATE, k - 1), at.to_z(k))
+        return remote(ref, ref, self.zs, (LATE, k - 1), at.to_z(k), (LATE,))
+
+    def late_core(self, k, mine=True):
+        at = self.at
+        ref = self.g.at[LATE, at.below(k), :, at.c if mine else at.oc]
+        return remote(ref, ref, self.cs, (LATE + k,), at.to_c)
 
     def late_z(self):
         for copy in self.p2_copies(LATE, 0, False):
             copy.wait_recv()
         for k in range(1, NZ):
             self.late_copy(k).start()
-
-    def late_cross(self):
-        for k in range(1, NZ):
-            self.late_copy(k, False).wait_recv()
-        self.c_copy(LATE).start()
-
-    def arrive(self, ch):
-        self.c_copy(ch, False).wait_recv()
+        self.late_core(0).start()
+
+    def late_cross(self, k):
+        self.late_copy(k, False).wait_recv()
+        self.late_core(k).start()
+
+    def late_arrive(self, k):
+        self.late_core(k, False).wait_recv()
+
+    def sent(self, ref, sem):
+        pltpu.make_async_remote_copy(
+            src_ref=ref, dst_ref=ref, send_sem=sem, recv_sem=sem, device_id=self.at.to_c,
+            device_id_type=pl.DeviceIdType.MESH,
+        ).wait_send()
 
     def drain(self, ch):
-        for k in range(1, NZ):
-            self.z_copy(ch, k).wait_send()
-
-        def one(k):
-            for copy in self.p1_copies(ch, k) + self.p2_copies(ch, k):
-                copy.wait_send()
-
-        loop(NZ, one)
+        self.sent(self.g.at[ch, 0:3, 0, 0, 0], self.zs[0].at[ch])
+        self.sent(self.g.at[ch, :, :, 0, 0], self.p1[0].at[ch])
+        self.sent(self.g.at[ch, :, 0, 0, 0], self.p2[0].at[ch])
         self.c_copy(ch).wait_send()
 
     def late_drain(self):
-        for k in range(1, NZ):
-            self.late_copy(k).wait_send()
-        for copy in (*self.p1_copies(LATE, 0), *self.p2_copies(LATE, 0), self.c_copy(LATE)):
-            copy.wait_send()
+        self.sent(self.g.at[LATE, 0:3, :, 0], self.zs[0].at[LATE])
+        self.sent(self.g.at[LATE, 0:1, :, 0, 0], self.p1[0].at[LATE])
+        self.sent(self.g.at[LATE, 0:1, 0, 0, 0], self.p2[0].at[LATE])
+        for k in range(NZ):
+            self.late_core(k).wait_send()
 
 
 def fold(wide):
@@ -285,9 +309,10 @@
 
 
 class Scatter:
-    def __init__(self, at, s, r1, rd0, rd1, rx, ry, rz, early, cs, p2, p1, zs):
+    def __init__(self, at, s, r1, rd0, rd1, rx, ry, rz, early, earlier, sent, cs, p2, p1, zs):
         self.at, self.s = at, s
-        self.early = early
+        self.early, self.sent = early, sent
+        self.erd0, self.erd1, self.erx, self.ery = earlier
         self.r1, self.rd0, self.rd1, self.rx, self.ry, self.rz = r1, rd0, rd1, rx, ry, rz
         self.cs, self.p2, self.p1, self.zs = cs, p2, p1, zs
 
@@ -295,33 +320,47 @@
         at = self.at
         return remote(self.s.at[ch, :, :, at.oc], self.r1.at[ch], self.cs, (ch,), at.to_c)
 
-    def zs_of(self, ch, k):
-        return slice(None) if k is None else pl.ds(self.at.above(k), 1)
+    def some(self, ch, k):
+        if k is None:
+            return slice(None), ch
+        return pl.ds(self.at.above(k), 1), FINE[0] + NZ * FINE.index(ch) + k
 
     def p2_copies(self, ch, k=None):
-        at, some, index = self.at, self.zs_of(ch, k), k or 0
+        at = self.at
+        some, index = self.some(ch, k)
         head, tail = pl.ds(0, CUT), pl.ds(CUT, ROWS - CUT)
         corner = self.s.at[ch, some, at.ox, at.c, at.oy]
         return (
-            remote(corner.at[:, head], self.rd0.at[ch, some], self.p2, (ch, index, 0), at.to_x),
-            remote(corner.at[:, tail], self.rd1.at[ch, some], self.p2, (ch, index, 1), at.to_y),
+            remote(corner.at[:, head], self.rd0.at[ch - 1, some], self.p2, (index, 0), at.to_x, (ch,)),
+            remote(corner.at[:, tail], self.rd1.at[ch - 1, some], self.p2, (index, 1), at.to_y, (ch,)),
         )
 
     def p1_copies(self, ch, k=None):
-        at, some, index = self.at, self.zs_of(ch, k), k or 0
+        at = self.at
+        some, index = self.some(ch, k)
         return (
-            remote(self.s.at[ch, some, at.ox, at.c, at.y], self.rx.at[ch, some], self.p1, (ch, index, 0), at.to_x),
-            remote(self.s.at[ch, some, at.x, at.c, at.oy], self.ry.at[ch, some], self.p1, (ch, index, 1), at.to_y),
+            remote(self.s.at[ch, some, at.ox, at.c, at.y], self.rx.at[ch - 1, some], self.p1, (index, 0), at.to_x, (ch,)),
+            remote(self.s.at[ch, some, at.x, at.c, at.oy], self.ry.at[ch - 1, some], self.p1, (index, 1), at.to_y, (ch,)),
         )
 
     def z_copy(self, ch, k):
         at = self.at
         return remote(
-            self.s.at[ch, at.above(k), at.x, at.c, at.y], self.rz.at[ch, k - 1], self.zs, (ch, k - 1), at.to_z(k)
+            self.s.at[ch, at.above(k), at.x, at.c, at.y], self.rz.at[ch - 1, k - 1], self.zs, (ch, k - 1), at.to_z(k), (ch,)
         )
 
+    def first_copies(self):
+        at, s, r1 = self.at, self.s, self.r1
+        pieces = (
+            (s.at[1, :, at.ox, at.oc, at.oy], r1.at[1, :, at.ox, at.oy]),
+            (s.at[1, :, at.ox, at.oc, at.y], r1.at[1, :, at.ox, at.y]),
+            (s.at[1, :, at.x, at.oc], r1.at[1, :, at.x]),
+        )
+        return [remote(src, dst, self.cs, (index,), at.to_c) for (src, dst), index in zip(pieces, (1, CHUNKS, CHUNKS + 1))]
+
     def start(self, ch):
-        self.c_copy(ch).start()
+        for copy in self.first_copies() if ch == 1 else (self.c_copy(ch),):
+            copy.start()
 
     def add_core(self, ch, x, y):
         def one(z):
@@ -332,11 +371,14 @@
 
     def core(self, ch):
         at = self.at
-        self.c_copy(ch).wait_recv()
+        copies = self.first_copies() if ch == 1 else [self.c_copy(ch)]
+        copies[0].wait_recv()
         self.add_core(ch, at.ox, at.oy)
         for k in (1, 2, 3, 0) if ch in FINE else (None,):
             for copy in self.p2_copies(ch, k):
                 copy.start()
+        for copy in copies[1:]:
+            copy.wait_recv()
         self.add_core(ch, at.ox, at.y)
         self.add_core(ch, at.x, at.oy)
         self.add_core(ch, at.x, at.y)
@@ -355,7 +397,7 @@
         over_x.wait_recv()
 
         def first(z):
-            total = self.s[ch, z, at.x, at.c, at.oy, head].astype(F32) + self.rd0[ch, z].astype(F32)
+            total = self.s[ch, z, at.x, at.c, at.oy, head].astype(F32) + self.rd0[ch - 1, z].astype(F32)
             self.s[ch, z, at.x, at.c, at.oy, head] = total.astype(BF)
 
         self.over(k, first)
@@ -363,7 +405,7 @@
         over_y.wait_recv()
 
         def second(z):
-            total = self.s[ch, z, at.ox, at.c, at.y, tail].astype(F32) + self.rd1[ch, z].astype(F32)
+            total = self.s[ch, z, at.ox, at.c, at.y, tail].astype(F32) + self.rd1[ch - 1, z].astype(F32)
             self.s[ch, z, at.ox, at.c, at.y, tail] = total.astype(BF)
 
         self.over(k, second)
@@ -375,8 +417,8 @@
             copy.wait_recv()
 
         def one(z):
-            total = self.s[ch, z, at.x, at.c, at.y].astype(F32) + self.rx[ch, z].astype(F32)
-            total = total + self.ry[ch, z].astype(F32)
+            total = self.s[ch, z, at.x, at.c, at.y].astype(F32) + self.rx[ch - 1, z].astype(F32)
+            total = total + self.ry[ch - 1, z].astype(F32)
             self.s[ch, z, at.x, at.c, at.y] = total.astype(BF)
 
         self.over(k, one)
@@ -389,22 +431,21 @@
             self.z_copy(ch, k).wait_recv()
         total = self.s[ch, at.z, at.x, at.c, at.y].astype(F32)
         for k in range(NZ - 1):
-            total = total + self.rz[ch, k].astype(F32)
+            total = total + self.rz[ch - 1, k].astype(F32)
         return total
 
     def drain(self, ch):
-        self.c_copy(ch).wait_send()
-        for k in range(NZ) if ch in FINE else (None,):
-            for copy in (*self.p2_copies(ch, k), *self.p1_copies(ch, k)):
-                copy.wait_send()
-        for k in range(1, NZ):
-            self.z_copy(ch, k).wait_send()
+        for copy in self.first_copies() if ch == 1 else (self.c_copy(ch),):
+            copy.wait_send()
+        self.sent(self.s.at[ch, :, 0, 0, 0], self.p2[0].at[ch])
+        self.sent(self.s.at[ch, :, :, 0, 0], self.p1[0].at[ch])
+        self.sent(self.s.at[ch, 0:3, 0, 0, 0], self.zs[0].at[ch])
 
 
     def early_z(self):
         at = self.at
         return [
-            remote(self.s.at[0, at.above(k), :, at.c], self.early.at[k - 1], self.zs, (0, k - 1), at.to_z(k))
+            remote(self.s.at[0, at.above(k), :, at.c], self.early.at[k - 1], self.zs, (0, k - 1), at.to_z(k), (0,))
             for k in range(1, NZ)
         ]
 
@@ -412,15 +453,15 @@
         at = self.at
         head, tail = pl.ds(0, CUT), pl.ds(CUT, ROWS - CUT)
         return (
-            remote(self.s.at[0, at.z, at.ox, at.c, at.oy, head], self.rd0.at[0, 0], self.p2, (0, 0, 0), at.to_x),
-            remote(self.s.at[0, at.z, at.ox, at.c, at.oy, tail], self.rd1.at[0, 0], self.p2, (0, 0, 1), at.to_y),
+            remote(self.s.at[0, at.z, at.ox, at.c, at.oy, head], self.erd0, self.p2, (0, 0), at.to_x, (0,)),
+            remote(self.s.at[0, at.z, at.ox, at.c, at.oy, tail], self.erd1, self.p2, (0, 1), at.to_y, (0,)),
         )
 
     def early_p1(self):
         at = self.at
         return (
-            remote(self.s.at[0, at.z, at.ox, at.c, at.y], self.rx.at[0, 0], self.p1, (0, 0, 0), at.to_x),
-            remote(self.s.at[0, at.z, at.x, at.c, at.oy], self.ry.at[0, 0], self.p1, (0, 0, 1), at.to_y),
+            remote(self.s.at[0, at.z, at.ox, at.c, at.y], self.erx, self.p1, (0, 0), at.to_x, (0,)),
+            remote(self.s.at[0, at.z, at.x, at.c, at.oy], self.ery, self.p1, (0, 1), at.to_y, (0,)),
         )
 
     def early_core(self):
@@ -458,11 +499,11 @@
         to_x, to_y = self.early_p1()
         head, tail = pl.ds(0, CUT), pl.ds(CUT, ROWS - CUT)
         over_x.wait_recv()
-        total = self.s[0, at.z, at.x, at.c, at.oy, head].astype(F32) + self.rd0[0, 0].astype(F32)
+        total = self.s[0, at.z, at.x, at.c, at.oy, head].astype(F32) + self.erd0[...].astype(F32)
         self.s[0, at.z, at.x, at.c, at.oy, head] = total.astype(BF)
         to_y.start()
         over_y.wait_recv()
-        total = self.s[0, at.z, at.ox, at.c, at.y, tail].astype(F32) + self.rd1[0, 0].astype(F32)
+        total = self.s[0, at.z, at.ox, at.c, at.y, tail].astype(F32) + self.erd1[...].astype(F32)
         self.s[0, at.z, at.ox, at.c, at.y, tail] = total.astype(BF)
         to_x.start()
 
@@ -470,12 +511,14 @@
         at = self.at
         for copy in self.early_p1():
             copy.wait_recv()
-        total = self.s[0, at.z, at.x, at.c, at.y].astype(F32) + self.rx[0, 0].astype(F32)
-        return total + self.ry[0, 0].astype(F32)
+        total = self.s[0, at.z, at.x, at.c, at.y].astype(F32) + self.erx[...].astype(F32)
+        return total + self.ery[...].astype(F32)
 
     def early_drain(self):
-        for copy in (self.c_copy(0), *self.early_z(), *self.early_p2(), *self.early_p1()):
-            copy.wait_send()
+        self.c_copy(0).wait_send()
+        self.sent(self.s.at[0, 0:1, 0, 0, 0], self.p2[0].at[0])
+        self.sent(self.s.at[0, 0:1, :, 0, 0], self.p1[0].at[0])
+        self.sent(self.s.at[0, 0:3, :, 0], self.zs[0].at[0])
 
 
 def unfold(total, unit):
@@ -625,27 +668,34 @@
 
 def layer_kernel(
     stride,
-    q, k, v, o, inner, outer, small, hidden, grad, mask,
+    q, k, v, o, inner, outer, qb, vb, ob, g1, s1, ub, g2, s2, inner_bias, pad, hidden, grad, lengths,
     out, igrad, dq, dk, dv, do, di, du, dsmall, saved,
-    g, gv, wd, u, page, cot, dead, hid, qkv, outp, xt, hidt, ctxt,
+    g, gv, wd, u, page, cot, dead, mask, small, hid, qkv, outp, xt, hidt, ctxt, actt,
     n1, inv1, acc1, acc2, dst, bias, vec, ib, vg, ibg,
-    sv, r1, rd0, rd1, rx, ry, rz, early, vc, vx, vy, vz,
+    sv, r1, rd0, rd1, rx, ry, rz, early, erd0, erd1, erx, ery, vc, vx, vy, vz,
     zs, zr, p1s, p1r, p2s, p2r, cs, cr, vs, vr, es, er,
-    css, csr, q2s, q2r, q1s, q1r, zss, zsr, ws, wr, loads, saves,
+    csr, q2r, q1r, zsr, wr, loads, saves, stores,
 ):
     at = Place(stride)
     gather = Gather(at, g, (zs, zr), (p1s, p1r), (p2s, p2r), (cs, cr))
     scatter = Scatter(
-        at, g, r1, rd0, rd1, rx, ry, rz, early, (css, csr), (q2s, q2r), (q1s, q1r), (zss, zsr)
+        at, g, r1, rd0, rd1, rx, ry, rz, early, (erd0, erd1, erx, ery), gather.sent, (cs, csr), (p2s, q2r), (p1s, q1r), (zs, zsr)
     )
-    vector = VectorScatter(at, sv, vc, vx, vy, vz, (ws, wr))
+    vector = VectorScatter(at, sv, vc, vx, vy, vz, (vs, wr))
 
     def put(ch, value):
         g[ch, at.z, at.x, at.c, at.y] = value
 
     at.hail()
     pack_weights((q, k, v, o, inner, outer), put)
-    gv[at.z, at.x, at.c, at.y] = small[...]
+    small[...] = jnp.zeros_like(small)
+    for i, ref in enumerate((qb, vb, ob, g1, s1, ub, g2, s2, inner_bias)):
+        small[i : i + 1, 0 : ref.shape[-1]] = ref[...].astype(F32).reshape(1, ref.shape[-1])
+    gv[at.z, at.x, at.c, at.y] = small[...].astype(BF)
+    position = lax.broadcasted_iota(jnp.int32, (8, 256), 1) + at.y * 256
+    for i in range(2):
+        live = (position < lengths[i]) & (jnp.broadcast_to(pad[i : i + 1], (8, 256)) == 1)
+        mask[i] = jnp.where(live, 0.0, NEG_FILL)
     own = pl.ds(pl.multiple_of(at.y * 256, 256), 256)
     theirs = pl.ds(pl.multiple_of(at.oy * 256, 256), 256)
     local = [
@@ -794,29 +844,46 @@
             u[rows, pl.ds(pl.multiple_of(3072 + 384 * i, 384), 384)] = (cdf + value * density).astype(BF)
 
         loop(8, one)
-
-    def outer_half(half):
-        cols = slice(COLS * half, COLS * half + COLS)
-        weight = g[4 + half].reshape(8 * COLS, COLS)
-        acc1[:, cols] = product(u[:, 0:3072], weight)
+        actt[cols, :] = u[:, cols].T
+
+    def outer_left():
+        acc1[:, 0:COLS] = product(u[:, 0:3072], g[4].reshape(8 * COLS, COLS))
+
+    def outer_right(step):
+        z = at.below(step)
+        value = product(u[:, tile(z, 768)], g[LATE, z].reshape(2 * COLS, COLS))
+        acc1[:, COLS:] = value if step == 0 else acc1[:, COLS:] + value
+
+    def cotangent():
+        vg[...] = jnp.zeros_like(vg)
+
+        def one(i):
+            rows = tile(i, 64)
+            dy = cot[rows, :].astype(F32)
+            vg[S2 : S2 + 1] += column(dy)
+            bias[rows, :] = jnp.broadcast_to(mean(dy * vec[G2 : G2 + 1]), (64, 128))
+
+        loop(8, one)
 
     def second_norm(i):
-        rows = tile(i, 64)
-        second = hid[rows, :].astype(F32) + (acc1[rows, :] + vec[UB : UB + 1])
-        center = second - mean(second)
-        inverse = lax.rsqrt(mean(center * center) + EPSILON)
-        normed = center * inverse
         gain = vec[G2 : G2 + 1]
-        outp[rows, :] = (normed * gain + vec[S2 : S2 + 1]).astype(BF)
-        dy = cot[rows, :].astype(F32)
-        vg[G2 : G2 + 1] += column(dy * normed)
-        vg[S2 : S2 + 1] += column(dy)
-        scaled = dy * gain
-        back = inverse * (scaled - mean(scaled) - normed * mean(scaled * normed))
-        acc2[rows, :] = back
-        low = back.astype(BF)
-        page[rows, :] = low
-        vg[UB : UB + 1] += column(low.astype(F32))
+        sums = [jnp.zeros((1, WIDTH), F32)] * 2
+        for part in range(2):
+            rows = tile(2 * i + part, 64)
+            second = hid[rows, :].astype(F32) + (acc1[rows, :] + vec[UB : UB + 1])
+            center = second - mean(second)
+            inverse = lax.rsqrt(mean(center * center) + EPSILON)
+            normed = center * inverse
+            outp[rows, :] = (normed * gain + vec[S2 : S2 + 1]).astype(BF)
+            dy = cot[rows, :].astype(F32)
+            product_normed = dy * normed
+            back = inverse * (dy * gain - bias[rows, 0:1] - normed * mean(product_normed * gain))
+            acc2[rows, :] = back
+            low = back.astype(BF)
+            page[rows, :] = low
+            sums = [sums[0] + column(product_normed), sums[1] + column(low.astype(F32))]
+        vg[G2 : G2 + 1] += sums[0]
+        vg[UB : UB + 1] += sums[1]
 
     play(
         FORWARD,
@@ -829,6 +896,9 @@
             "arrive": gather.arrive,
             "late_z": gather.late_z,
             "late_cross": gather.late_cross,
+            "late_arrive": gather.late_arrive,
+            "plane_all": gather.plane_all,
+            "cotangent": cotangent,
             "vector_z": vector_z,
             "vector_x": vector_x,
             "vector_y": vector_y,
@@ -843,17 +913,21 @@
             "queries_keys": queries_keys,
             "values": lambda: loop(3, vals),
             "after_attention": after_attention,
-            "outer": outer_half,
+            "outer_left": outer_left,
+            "outer_right": outer_right,
         },
         {"attend": attend, "feed": feed, "feed_on": lambda i: feed(i + 4)},
     )
-    vg[...] = jnp.zeros_like(vg)
-    loop(8, second_norm)
+    loop(4, second_norm)
 
     low = page
     keep = pltpu.make_async_copy(outp.at[own], out.at[at.y], loads.at[0])
-    loop(CHUNKS - 1, gather.drain)
+    for ch in range(LATE):
+        gather.drain(ch)
     gather.late_drain()
+
+    for copy in vzs + [vxs, vys, vcs]:
+        copy.wait_send()
 
     def out_start():
         out_over.start()
@@ -861,26 +935,24 @@
 
     def outer_grad(half, slot):
         def one(i):
-            z, x = i // 2, rem(i, 2)
             cols = slice(COLS * half, COLS * half + COLS)
-            value = product_left(u[:, tile(i, 384)], low[:, cols]).astype(BF)
-            g[slot, z, x] = value.reshape(NC, NY, ROWS, COLS)
-
-        loop(8, one)
+            value = product(actt[tile(i, 1536), :], low[:, cols]).astype(BF)
+            g[slot, pl.ds(2 * i, 2)] = value.reshape(2, NX, NC, NY, ROWS, COLS)
+
+        loop(2, one)
 
     def load(part):
         cols = pl.ds(3072 * part, 3072)
         return pltpu.make_async_copy(saved.at[:, cols], u.at[:, cols], loads.at[1])
 
     def inner_back(i):
-        z, x = i // 2, rem(i, 2)
-        value = product_right(low[:, 0:COLS], g[4, z, x].reshape(COLS, COLS))
-        value = value + product_right(low[:, COLS:], g[5, z, x].reshape(COLS, COLS))
-        cols = pl.ds(pl.multiple_of(3072 + 384 * i, 384), 384)
+        weight = [g[4 + half, i].reshape(2 * COLS, COLS) for half in range(2)]
+        value = product_right(low[...], jnp.concatenate(weight, axis=1))
+        cols = pl.ds(pl.multiple_of(3072 + 768 * i, 768), 768)
         value = (value * u[:, cols].astype(F32)).astype(BF)
         u[:, cols] = value
         total = column(value.astype(F32))
-        ibg[:, tile(i, 384)] = jnp.broadcast_to(total, (8, 384))
+        ibg[:, tile(i, 768)] = jnp.broadcast_to(total, (8, 768))
 
     def weight_grad(slot, unit, left, right):
         def one(i):
@@ -957,19 +1029,28 @@
         grad_over.start()
         keep_in.start()
 
+    def result(index):
+        if index < 2:
+            rows, cols = pl.ds(0, ROWS), pl.ds(COLS * (1 - index), COLS)
+            target = du.at[:, cols]
+        else:
+            rows, cols = pl.ds(ROWS + 24 * (index - 2), 24), pl.ds(0, WIDTH)
+            target = di.at[:, pl.ds(WIDTH * (index - 2), WIDTH)] if index < 6 else (dv, do, dq, dk)[index - 6]
+        place = acc1.at[rows, cols]
+        return place, pltpu.make_async_copy(place, target, stores.at[index])
+
+    def store(index, value):
+        place, copy = result(index)
+        place[...] = value
+        copy.start()
+
     def finish(n):
         total = scatter.finish(n) if n else scatter.early_finish()
         if n < 2:
-            half = 1 - n
-            du[:, COLS * half : COLS * half + COLS] = total
-        elif n < 4:
-            for unit in range(2):
-                index = 2 * (n - 2) + unit
-                di[:, WIDTH * index : WIDTH * (index + 1)] = unfold(total, unit)
+            store(n, total)
         else:
-            first, second = (dv, do) if n == 4 else (dq, dk)
-            first[...] = unfold(total, 0)
-            second[...] = unfold(total, 1)
+            store(2 * n - 2, unfold(total, 0))
+            store(2 * n - 1, unfold(total, 1))
 
     def vector_finish():
         dsmall[...] = vector.finish()
@@ -1029,13 +1110,15 @@
     )
     keep.wait()
     keep_in.wait()
+    for index in range(10):
+        result(index)[1].wait()
     out_over.wait_recv()
     grad_over.wait_recv()
     for n in range(1, CHUNKS):
         scatter.drain(n)
     scatter.early_drain()
     vector.drain()
-    for copy in vzs + [vxs, vys, vcs] + swaps:
+    for copy in swaps:
         copy.wait_send()
 
 
@@ -1062,8 +1145,8 @@
     return pl.pallas_call(
         partial(layer_kernel, stride),
         out_shape=tuple(tokens + grads + [shape(512, 12 * 512, kind=BF)]),
-        in_specs=[vmem] * 7 + [hbm, hbm, vmem],
-        out_specs=tuple([hbm] * 2 + [vmem] * len(grads) + [hbm]),
+        in_specs=[vmem] * 16 + [hbm, hbm, pl.BlockSpec(memory_space=pltpu.SMEM)],
+        out_specs=tuple([hbm] * 8 + [vmem, hbm]),
         scratch_shapes=[
             low(CHUNKS, NZ, NX, NC, NY, ROWS, COLS),
             low(NZ, NX, NC, NY, 16, 128),
@@ -1072,12 +1155,15 @@
             low(512, WIDTH),
             low(512, WIDTH),
             full(2, 8, 256),
+            full(2, 8, 256),
+            full(16, 128),
             low(512, WIDTH),
             low(512, 3 * WIDTH),
             low(512, WIDTH),
             low(WIDTH, 512),
             low(WIDTH, 512),
             low(WIDTH, 512),
+            low(4 * WIDTH, 512),
             full(512, WIDTH),
             full(512, 128),
             full(512, WIDTH),
@@ -1090,29 +1176,34 @@
             full(8, 4 * WIDTH),
             full(NZ, NX, NC, NY, 16, 128),
             low(CHUNKS, NZ, NX, NY, ROWS, COLS),
-            low(CHUNKS, NZ, CUT, COLS),
-            low(CHUNKS, NZ, ROWS - CUT, COLS),
-            low(CHUNKS, NZ, ROWS, COLS),
-            low(CHUNKS, NZ, ROWS, COLS),
-            low(CHUNKS, NZ - 1, ROWS, COLS),
+            low(CHUNKS - 1, NZ, CUT, COLS),
+            low(CHUNKS - 1, NZ, ROWS - CUT, COLS),
+            low(CHUNKS - 1, NZ, ROWS, COLS),
+            low(CHUNKS - 1, NZ, ROWS, COLS),
+            low(CHUNKS - 1, NZ - 1, ROWS, COLS),
             low(NZ - 1, NX, NY, ROWS, COLS),
+            low(CUT, COLS),
+            low(ROWS - CUT, COLS),
+            low(ROWS, COLS),
+            low(ROWS, COLS),
             full(NZ, NX, NY, 16, 128),
             full(NZ, NY, 16, 128),
             full(NZ, 16, 128),
             full(NZ - 1, 16, 128),
-            *pair(CHUNKS, NZ - 1),
-            *pair(CHUNKS, NZ, 2),
-            *pair(CHUNKS, NZ, 2),
-            *pair(CHUNKS),
+            dma((CHUNKS,)), dma((CHUNKS, NZ - 1)),
+            dma((CHUNKS,)), dma((G_STEPS, 2)),
+            dma((CHUNKS,)), dma((G_STEPS, 2)),
+            *pair(LATE + NZ),
             *pair(6),
             *pair(5),
-            *pair(CHUNKS),
-            *pair(CHUNKS, NZ, 2),
-            *pair(CHUNKS, NZ, 2),
-            *pair(CHUNKS, NZ - 1),
-            *pair(6),
+            dma((CHUNKS + 2,)),
+            dma((S_STEPS, 2)),
+            dma((S_STEPS, 2)),
+            dma((CHUNKS, NZ - 1)),
+            dma((6,)),
             dma((2,)),
             dma((6,)),
+            dma((10,)),
         ],
         compiler_params=pltpu.CompilerParams(
             collective_id=0, has_side_effects=True, vmem_limit_bytes=VMEM_LIMIT
@@ -1176,26 +1267,12 @@
 ):
     coarse = partial(own_part, stride=stride)
     fine = partial(fine_part, stride=stride)
-    place = lax.axis_index("blk")
-    segment = hidden_in.shape[1]
-    positions = place * segment + jnp.arange(segment, dtype=jnp.int32)
-    live = (positions[None, :] < page_lengths[:, None]) & (pad_mask == 1)
-    mask = jnp.where(live, 0.0, NEG_FILL).astype(F32)
-    mask = jnp.broadcast_to(mask[:, None, :], (2, 8, segment))
+    weights = (query_weight, key_weight, value_weight, output_weight, inner_weight, outer_weight)
     vectors = (
-        query_bias, value_bias, output_bias, first_gain, first_shift, outer_bias, second_gain, second_shift,
+        query_bias, value_bias, output_bias, first_gain, first_shift, outer_bias, second_gain, second_shift, inner_bias,
     )
-    small = jnp.stack([coarse(v) for v in vectors])
-    small = jnp.concatenate(
-        [
-            jnp.pad(small, ((0, 0), (0, 104))),
-            jnp.pad(coarse(inner_bias)[None, :], ((0, 7), (0, 32))),
-        ]
-    )
-    weights = [
-        coarse(v) for v in (query_weight, key_weight, value_weight, output_weight, inner_weight, outer_weight)
-    ]
-    *large, dsmall, _ = layer_call(stride, (*weights, small, hidden_in, out_grad, mask))
+    parts = [coarse(v) for v in weights + vectors]
+    *large, dsmall, _ = layer_call(stride, (*parts, pad_mask, hidden_in, out_grad, page_lengths))
     output, input_grad, *grads = hand_out(large, dsmall)
     dq, dk, dv, do, di, du, qbg, vbg, obg, g1g, s1g, ubg, g2g, s2g, ibg = [fine(v) for v in grads]
     return (

time: 174 us -> 157 us (0.902)
  Pallas kernels: 170 us -> 156 us
  other arithmetic: 2.01 us -> 0 us
    pallas_call x1, Pallas kernels: 166 us -> 152 us  [layer_call(): pl.pallas_call(partial(layer_kernel, stride), out_shape=tuple(tokens + gr...]
where the time goes in v2:
time: 157 us
  Pallas kernels  156 us (99%)
    pallas_call x1, Pallas kernels, layer_call(): pl.pallas_call(partial(layer_kernel, stride), out_shape=tuple(tokens + gr...  152 us
    pallas_call x1, Pallas kernels, hand_out(): pl.pallas_call(hand_out_kernel, out_shape=tuple([jax.ShapeDtypeStruct(v.s...  3.96 us

profile of v2, /device:TPU:0, one launch (start us, length us, event | category | flops | bytes accessed | tf_op | source)
XLA Modules:
  0.0 156.8 jit_solution(13121372106283071296)
XLA Ops:
  0.7 152.0 %layer.1 = (bf16[2,256,768]{2,1,0:T(8,128)(2,1)}, bf16[2,256,768]{2,1,0:T(8,128)(2,1)}, f32[24,768]{1,0:T(8,128)}, f32[24,768]{1,0:T(8,128)}, f32[24,768]{1,0:T(...) custom-call(bf16[24,768]{1,0:T(8,128)(2,1)} %q.1, ...), custom_call_target="tpu_custom_call" | custom-call | tf_op jit(solution)/shard_map/layer/pallas_call | solution.py:1145
  152.7 4.0 %hand_out.1 = (bf16[2,256,768]{2,1,0:T(8,128)(2,1)}, bf16[2,256,768]{2,1,0:T(8,128)(2,1)}, f32[24,768]{1,0:T(8,128)}, f32[24,768]{1,0:T(8,128)}, f32[24,768]{1,0...) custom-call(bf16[2,256,768]{2,1,0:T(8,128)(2,1)} %get-tuple-element., ...), custom_call_target="tpu_custom_call" | custom-call | tf_op jit(solution)/shard_map/hand_out/pallas_call | solution.py:1235

commit v3 on v2

--- a/solution.py
+++ b/solution.py
@@ -18,38 +18,43 @@
 LATE = 5
 FINE_G, COARSE = (0, 1), (2, 3, 4)
 G_STEPS = NZ * len(FINE_G) + len(COARSE) + 1
-CUT = 64
+G_ALONG = len(COARSE) + (NZ - 1) * (len(FINE_G) + 1)
 WIDTH = 768
+CUTS_G = (64, 80, 48, 48, 64, 80)
+CUTS_S = (32, 48, 32, 48, 48, 80)
 FINE = (4, 5)
 S_STEPS = FINE[0] + NZ * len(FINE)
 BF, F32 = jnp.bfloat16, jnp.float32
 VMEM_LIMIT = 63 * 2**20
 
 FORWARD = (
-    "vector_z", "own 1", "z 0", "own 5", "page", "z 1", "turn 1 0", "own 0", "z 2", "plane 0 2", "vector_x",
-    "plane 0 1", "z 3", "turn 5 0", "plane 0 3", "plane 1 1", "plane 1 2", "plane 1 3", "turn 0 2", "vector_y",
-    "turn 0 1", "turn 0 0", "turn 0 3", "turn 1 1", "turn 1 2", "z 4", "turn 1 3", "plane_all 2", "vector_c",
-    "vector_wait", "page_wait", "late_z", "cross 0", "cross 1", "plane_all 3", "arrive 0", "prepare",
-    "arrive 1", "late_arrive 0", "unpack 1", "unpack 0", "queries_keys", "turn 2", "values", "attend 0",
-    "plane_all 4", "attend 1", "turn 3", "attend 2", "attend 3", "cross 2", "attend 4", "attend 5",
-    "after_attention", "arrive 2", "turn 4", "grad", "unpack 2", "feed 0", "late_cross 1", "feed 1", "cross 3",
-    "feed 2", "late_arrive 1", "feed 3", "arrive 3", "unpack 3", "late_cross 3", "late_cross 2", "feed_on 4",
-    "cross 4", "feed_on 5", "feed_on 6", "late_arrive 2", "feed_on 7", "arrive 4", "outer_left",
-    "outer_right 0", "grad_wait", "outer_right 1", "late_arrive 3", "cotangent", "outer_right 2",
+    "own 5", "own 1", "vector_z", "z 0", "z 1", "turn 5 0", "own 0", "page", "turn 1 0", "plane 0 1",
+    "vector_x", "z 2", "plane 0 3", "plane 0 2", "plane 1 1", "plane 1 2", "turn 0 1", "turn 0 0", "z 3",
+    "plane 1 3", "turn 1 1", "page_wait", "turn 0 3", "vector_y", "turn 1 2", "turn 0 2", "turn 1 3", "z 4",
+    "plane_all 2", "vector_c", "cross 0", "vector_wait", "cross 1", "prepare", "arrive 0", "late_z", "arrive 1",
+    "plane_all 3", "unpack 0", "queries_keys", "turn 2", "unpack 1", "values", "attend 0", "attend 1",
+    "attend 2", "plane_all 4", "attend 3", "attend 4", "turn 3", "cross 2", "attend 5", "after_attention",
+    "arrive 2", "unpack 2", "feed 0", "turn 4", "grad", "feed 1", "late_arrive 0", "cross 3", "feed 2",
+    "feed 3", "arrive 3", "unpack 3", "feed_on 4", "late_cross 1", "cross 4", "late_cross 2", "late_cross 3",
+    "feed_on 5", "feed_on 6", "feed_on 7", "arrive 4", "outer_left", "outer_right 0", "late_arrive 1",
+    "late_arrive 3", "outer_right 1", "late_arrive 2", "outer_right 2", "grad_wait", "cotangent",
     "outer_right 3",
 )
 BACKWARD = (
-    "out", "outer_first", "start 1", "outer_second", "start 0", "inner_back 0", "core 1", "inner_back 1",
-    "early_core", "inner_back 2", "inner_back 3", "inner_grad 0", "diagonal 1", "inner_grad 1", "start 2",
-    "inner_grad 2", "inner_grad 3", "hidden_back 0", "start 3", "hidden_back 1", "hidden_back 2", "core 2",
-    "first_back", "output_grad", "core 3", "context_back", "diagonal 2", "attend_back 0", "plane 1",
-    "attend_back 1", "attend_back 2", "diagonal 3", "attend_back 3", "attend_back 4", "attend_back 5",
-    "value_grad", "start 4", "key_grad", "query_grad", "start 5", "sums", "plane 2", "core 4", "core 5",
-    "diagonal 4 2", "early_plane", "plane 3", "diagonal 4 0", "gather_vectors", "vector", "diagonal 4 3",
-    "diagonal 5 3", "vector_core", "diagonal 5 2", "early_diagonal", "finish 1", "input_back 0", "diagonal 4 1",
-    "plane 4 2", "diagonal 5 1", "diagonal 5 0", "finish 3", "plane 4 3", "plane 4 0", "plane 5 3",
-    "input_back 1", "vector_x", "input_back 2", "grad", "plane 5 2", "finish 2", "vector_y", "plane 4 1",
-    "finish 0", "plane 5 1", "vector_finish", "plane 5 0", "finish 4", "finish 5",
+    "out", "outer_second 2", "outer_second 1", "outer_first 0", "early_start 2", "start_first 0",
+    "outer_first 1", "inner_back 0", "outer_second 3", "early_start 1", "outer_first 2", "outer_first 3",
+    "early_core 2", "core_first", "start_first 2", "inner_back 1", "start_first 1", "outer_second 0",
+    "inner_back 2", "inner_back 3", "core_rest", "early_start 3", "inner_grad 0", "early_start 0",
+    "early_core 1", "diagonal 1", "inner_grad 1", "early_core 0", "early_core 3", "start 2", "inner_grad 2",
+    "inner_grad 3", "hidden_back 0", "start 3", "core 2", "hidden_back 1", "hidden_back 2", "first_back",
+    "core 3", "diagonal 2", "context_back", "attend_back 0", "attend_back 1", "attend_back 2", "plane 1",
+    "output_grad", "early_plane", "diagonal 3", "attend_back 3", "attend_back 4", "attend_back 5", "value_grad",
+    "start 4", "early_diagonal", "key_grad", "query_grad", "sums", "plane 3", "start 5", "core 4",
+    "gather_vectors", "diagonal 4 1", "vector", "plane 2", "finish 1", "diagonal 4 2", "core 5", "input_back 0",
+    "diagonal 4 3", "plane 4 2", "vector_core", "input_back 1", "plane 4 1", "diagonal 5 1", "diagonal 5 2",
+    "diagonal 5 3", "diagonal 4 0", "finish 3", "diagonal 5 0", "input_back 2", "plane 4 3", "finish 0",
+    "vector_x", "grad", "plane 5 1", "plane 5 2", "finish 2", "plane 5 3", "plane 5 0", "vector_y", "plane 4 0",
+    "finish 4", "finish 5", "vector_finish",
 )
 
 
@@ -124,6 +129,10 @@
     lax.fori_loop(0, count, step, 0)
 
 
+def cut(rows):
+    return pl.ds(0, rows), pl.ds(rows, ROWS - rows)
+
+
 class Gather:
     def __init__(self, at, blocks, zs, p1, p2, cs):
         self.at, self.g = at, blocks
@@ -133,7 +142,12 @@
         at = self.at
         z = at.z if mine else at.below(k)
         ref = self.g.at[ch, z, at.x, at.c, at.y]
-        return remote(ref, ref, self.zs, (ch, k - 1), at.to_z(k), (ch,))
+        return remote(ref, ref, self.zs, self.along(ch, k), at.to_z(k), (ch,))
+
+    def along(self, ch, k):
+        if ch in COARSE:
+            return (ch - COARSE[0],)
+        return (len(COARSE) + (NZ - 1) * (FINE_G + (LATE,)).index(ch) + k - 1,)
 
     def some(self, ch, k):
         if ch in COARSE:
@@ -153,19 +167,15 @@
             remote(over_y, over_y, self.p1, (index, 1), at.to_y, (ch,)),
         )
 
-    def p2_copies(self, ch, k, mine=True):
-        at = self.at
-        z, index = self.some(ch, k)
-        head, tail = pl.ds(0, CUT), pl.ds(CUT, ROWS - CUT)
-        if mine:
-            over_x = self.g.at[ch, z, at.x, at.c, at.oy, head]
-            over_y = self.g.at[ch, z, at.ox, at.c, at.y, tail]
-        else:
-            over_x = self.g.at[ch, z, at.ox, at.c, at.oy, head]
-            over_y = self.g.at[ch, z, at.ox, at.c, at.oy, tail]
+    def p2_copies(self, ch, k):
+        at = self.at
+        z, _ = self.some(ch, k)
+        head, tail = cut(CUTS_G[ch])
+        over_x = self.g.at[ch, z, at.x, at.c, at.oy, head]
+        over_y = self.g.at[ch, z, at.ox, at.c, at.y, tail]
         return (
-            remote(over_x, over_x, self.p2, (index, 0), at.to_x, (ch,)),
-            remote(over_y, over_y, self.p2, (index, 1), at.to_y, (ch,)),
+            remote(over_x, over_x, self.p2, (ch,), at.to_x),
+            remote(over_y, over_y, self.p2, (ch,), at.to_y),
         )
 
     def c_copy(self, ch, mine=True):
@@ -187,8 +197,7 @@
             copy.start()
 
     def plane_all(self, ch):
-        for k in range(1, NZ):
-            self.z_copy(ch, k, False).wait_recv()
+        self.got(self.g.at[ch, 0:3, 0, 0, 0], self.zs[1].at[self.along(ch, 1)])
         for copy in self.p1_copies(ch, 0):
             copy.start()
 
@@ -201,9 +210,7 @@
         over_y.start()
 
     def cross(self, ch):
-        for k in range(NZ) if ch in FINE_G else (0,):
-            for copy in self.p2_copies(ch, k, False):
-                copy.wait_recv()
+        self.got(self.g.at[ch, :, 0, 0, 0], self.p2[1].at[ch])
         self.c_copy(ch).start()
 
     def arrive(self, ch):
@@ -213,7 +220,7 @@
     def late_copy(self, k, mine=True):
         at = self.at
         ref = self.g.at[LATE, at.z if mine else at.below(k), :, at.c]
-        return remote(ref, ref, self.zs, (LATE, k - 1), at.to_z(k), (LATE,))
+        return remote(ref, ref, self.zs, self.along(LATE, k), at.to_z(k), (LATE,))
 
     def late_core(self, k, mine=True):
         at = self.at
@@ -221,8 +228,7 @@
         return remote(ref, ref, self.cs, (LATE + k,), at.to_c)
 
     def late_z(self):
-        for copy in self.p2_copies(LATE, 0, False):
-            copy.wait_recv()
+        self.got(self.g.at[LATE, 0:1, 0, 0, 0], self.p2[1].at[LATE])
         for k in range(1, NZ):
             self.late_copy(k).start()
         self.late_core(0).start()
@@ -234,11 +240,17 @@
     def late_arrive(self, k):
         self.late_core(k, False).wait_recv()
 
-    def sent(self, ref, sem):
-        pltpu.make_async_remote_copy(
+    def all_of(self, ref, sem):
+        return pltpu.make_async_remote_copy(
             src_ref=ref, dst_ref=ref, send_sem=sem, recv_sem=sem, device_id=self.at.to_c,
             device_id_type=pl.DeviceIdType.MESH,
-        ).wait_send()
+        )
+
+    def sent(self, ref, sem):
+        self.all_of(ref, sem).wait_send()
+
+    def got(self, ref, sem):
+        self.all_of(ref, sem).wait_recv()
 
     def drain(self, ch):
         self.sent(self.g.at[ch, 0:3, 0, 0, 0], self.zs[0].at[ch])
@@ -309,16 +321,19 @@
 
 
 class Scatter:
-    def __init__(self, at, s, r1, rd0, rd1, rx, ry, rz, early, earlier, sent, cs, p2, p1, zs):
+    def __init__(self, at, s, r1, rd, rx, ry, rz, early, earlier, sent, got, cs, p2, p1, zs):
         self.at, self.s = at, s
-        self.early, self.sent = early, sent
-        self.erd0, self.erd1, self.erx, self.ery = earlier
-        self.r1, self.rd0, self.rd1, self.rx, self.ry, self.rz = r1, rd0, rd1, rx, ry, rz
+        self.early, self.sent, self.got = early, sent, got
+        self.erd, self.erx, self.ery = earlier
+        self.r1, self.rd, self.rx, self.ry, self.rz = r1, rd, rx, ry, rz
         self.cs, self.p2, self.p1, self.zs = cs, p2, p1, zs
 
+    def slot(self, ch):
+        return 1 if ch == CHUNKS - 1 else ch
+
     def c_copy(self, ch):
         at = self.at
-        return remote(self.s.at[ch, :, :, at.oc], self.r1.at[ch], self.cs, (ch,), at.to_c)
+        return remote(self.s.at[ch, :, :, at.oc], self.r1.at[self.slot(ch)], self.cs, (ch,), at.to_c)
 
     def some(self, ch, k):
         if k is None:
@@ -328,25 +343,25 @@
     def p2_copies(self, ch, k=None):
         at = self.at
         some, index = self.some(ch, k)
-        head, tail = pl.ds(0, CUT), pl.ds(CUT, ROWS - CUT)
+        head, tail = cut(CUTS_S[ch])
         corner = self.s.at[ch, some, at.ox, at.c, at.oy]
         return (
-            remote(corner.at[:, head], self.rd0.at[ch - 1, some], self.p2, (index, 0), at.to_x, (ch,)),
-            remote(corner.at[:, tail], self.rd1.at[ch - 1, some], self.p2, (index, 1), at.to_y, (ch,)),
+            remote(corner.at[:, head], self.rd.at[ch - 1, some, head], self.p2, (index, 0), at.to_x, (ch,)),
+            remote(corner.at[:, tail], self.rd.at[ch - 1, some, tail], self.p2, (index, 1), at.to_y, (ch,)),
         )
 
     def p1_copies(self, ch, k=None):
         at = self.at
         some, index = self.some(ch, k)
         return (
-            remote(self.s.at[ch, some, at.ox, at.c, at.y], self.rx.at[ch - 1, some], self.p1, (index, 0), at.to_x, (ch,)),
-            remote(self.s.at[ch, some, at.x, at.c, at.oy], self.ry.at[ch - 1, some], self.p1, (index, 1), at.to_y, (ch,)),
+            remote(self.s.at[ch, some, at.ox, at.c, at.y], self.rx.at[ch - 1, some], self.p1, (index,), at.to_x, (ch,)),
+            remote(self.s.at[ch, some, at.x, at.c, at.oy], self.ry.at[ch - 1, some], self.p1, (index,), at.to_y, (ch,)),
         )
 
     def z_copy(self, ch, k):
         at = self.at
         return remote(
-            self.s.at[ch, at.above(k), at.x, at.c, at.y], self.rz.at[ch - 1, k - 1], self.zs, (ch, k - 1), at.to_z(k), (ch,)
+            self.s.at[ch, at.above(k), at.x, at.c, at.y], self.rz.at[ch - 1, k - 1], self.zs, (ch,), at.to_z(k)
         )
 
     def first_copies(self):
@@ -359,29 +374,42 @@
         return [remote(src, dst, self.cs, (index,), at.to_c) for (src, dst), index in zip(pieces, (1, CHUNKS, CHUNKS + 1))]
 
     def start(self, ch):
-        for copy in self.first_copies() if ch == 1 else (self.c_copy(ch),):
-            copy.start()
+        self.c_copy(ch).start()
+
+    def start_first(self, piece):
+        self.first_copies()[piece].start()
 
     def add_core(self, ch, x, y):
         def one(z):
-            total = self.s[ch, z, x, self.at.c, y].astype(F32) + self.r1[ch, z, x, y].astype(F32)
+            total = self.s[ch, z, x, self.at.c, y].astype(F32) + self.r1[self.slot(ch), z, x, y].astype(F32)
             self.s[ch, z, x, self.at.c, y] = total.astype(BF)
 
         loop(NZ, one)
 
     def core(self, ch):
         at = self.at
-        copies = self.first_copies() if ch == 1 else [self.c_copy(ch)]
-        copies[0].wait_recv()
+        self.c_copy(ch).wait_recv()
         self.add_core(ch, at.ox, at.oy)
         for k in (1, 2, 3, 0) if ch in FINE else (None,):
             for copy in self.p2_copies(ch, k):
                 copy.start()
-        for copy in copies[1:]:
-            copy.wait_recv()
         self.add_core(ch, at.ox, at.y)
         self.add_core(ch, at.x, at.oy)
         self.add_core(ch, at.x, at.y)
+
+    def core_first(self):
+        self.first_copies()[0].wait_recv()
+        self.add_core(1, self.at.ox, self.at.oy)
+        for copy in self.p2_copies(1):
+            copy.start()
+
+    def core_rest(self):
+        at = self.at
+        for copy in self.first_copies()[1:]:
+            copy.wait_recv()
+        self.add_core(1, at.ox, at.y)
+        self.add_core(1, at.x, at.oy)
+        self.add_core(1, at.x, at.y)
 
     def over(self, k, work):
         if k is None:
@@ -393,11 +421,11 @@
         at = self.at
         over_x, over_y = self.p2_copies(ch, k)
         to_x, to_y = self.p1_copies(ch, k)
-        head, tail = pl.ds(0, CUT), pl.ds(CUT, ROWS - CUT)
+        head, tail = cut(CUTS_S[ch])
         over_x.wait_recv()
 
         def first(z):
-            total = self.s[ch, z, at.x, at.c, at.oy, head].astype(F32) + self.rd0[ch - 1, z].astype(F32)
+            total = self.s[ch, z, at.x, at.c, at.oy, head].astype(F32) + self.rd[ch - 1, z, head].astype(F32)
             self.s[ch, z, at.x, at.c, at.oy, head] = total.astype(BF)
 
         self.over(k, first)
@@ -405,7 +433,7 @@
         over_y.wait_recv()
 
         def second(z):
-            total = self.s[ch, z, at.ox, at.c, at.y, tail].astype(F32) + self.rd1[ch - 1, z].astype(F32)
+            total = self.s[ch, z, at.ox, at.c, at.y, tail].astype(F32) + self.rd[ch - 1, z, tail].astype(F32)
             self.s[ch, z, at.ox, at.c, at.y, tail] = total.astype(BF)
 
         self.over(k, second)
@@ -413,8 +441,8 @@
 
     def plane(self, ch, k=None):
         at = self.at
-        for copy in self.p1_copies(ch, k):
-            copy.wait_recv()
+        some = slice(None) if k is None else slice(0, 1)
+        self.got(self.s.at[ch, some, :, 0, 0], self.p1[1].at[self.some(ch, k)[1]])
 
         def one(z):
             total = self.s[ch, z, at.x, at.c, at.y].astype(F32) + self.rx[ch - 1, z].astype(F32)
@@ -427,8 +455,7 @@
 
     def finish(self, ch):
         at = self.at
-        for k in range(1, NZ):
-            self.z_copy(ch, k).wait_recv()
+        self.got(self.s.at[ch, 0:3, 0, 0, 0], self.zs[1].at[ch])
         total = self.s[ch, at.z, at.x, at.c, at.y].astype(F32)
         for k in range(NZ - 1):
             total = total + self.rz[ch - 1, k].astype(F32)
@@ -445,42 +472,51 @@
     def early_z(self):
         at = self.at
         return [
-            remote(self.s.at[0, at.above(k), :, at.c], self.early.at[k - 1], self.zs, (0, k - 1), at.to_z(k), (0,))
+            remote(self.s.at[0, at.above(k), :, at.c], self.early.at[k - 1], self.zs, (0,), at.to_z(k))
             for k in range(1, NZ)
         ]
 
     def early_p2(self):
         at = self.at
-        head, tail = pl.ds(0, CUT), pl.ds(CUT, ROWS - CUT)
+        head, tail = cut(CUTS_S[0])
         return (
-            remote(self.s.at[0, at.z, at.ox, at.c, at.oy, head], self.erd0, self.p2, (0, 0), at.to_x, (0,)),
-            remote(self.s.at[0, at.z, at.ox, at.c, at.oy, tail], self.erd1, self.p2, (0, 1), at.to_y, (0,)),
+            remote(self.s.at[0, at.z, at.ox, at.c, at.oy, head], self.erd.at[head], self.p2, (0, 0), at.to_x, (0,)),
+            remote(self.s.at[0, at.z, at.ox, at.c, at.oy, tail], self.erd.at[tail], self.p2, (0, 1), at.to_y, (0,)),
         )
 
     def early_p1(self):
         at = self.at
         return (
-            remote(self.s.at[0, at.z, at.ox, at.c, at.y], self.erx, self.p1, (0, 0), at.to_x, (0,)),
-            remote(self.s.at[0, at.z, at.x, at.c, at.oy], self.ery, self.p1, (0, 1), at.to_y, (0,)),
+            remote(self.s.at[0, at.z, at.ox, at.c, at.y], self.erx, self.p1, (0,), at.to_x),
+            remote(self.s.at[0, at.z, at.x, at.c, at.oy], self.ery, self.p1, (0,), at.to_y),
         )
 
-    def early_core(self):
-        at = self.at
-        self.c_copy(0).wait_recv()
+    def early_copy(self, k):
+        at = self.at
+        z = at.above(k)
+        index = CHUNKS + 1 + k if k else 0
+        return remote(self.s.at[0, z, :, at.oc], self.r1.at[0, z], self.cs, (index,), at.to_c)
+
+    def early_start(self, k):
+        self.early_copy(k).start()
+
+    def early_core(self, k):
+        at = self.at
+        self.early_copy(k).wait_recv()
+        z = at.above(k)
 
         def one(i):
-            z, x, y = i // (NX * NY), rem(i // NY, NX), rem(i, NY)
+            x, y = i // NY, rem(i, NY)
             total = self.s[0, z, x, at.c, y].astype(F32) + self.r1[0, z, x, y].astype(F32)
             self.s[0, z, x, at.c, y] = total.astype(BF)
 
-        loop(NZ * NX * NY, one)
-        for copy in self.early_z():
-            copy.start()
+        loop(NX * NY, one)
+        if k:
+            self.early_z()[k - 1].start()
 
     def early_plane(self):
         at = self.at
-        for copy in self.early_z():
-            copy.wait_recv()
+        self.got(self.s.at[0, 0:3, :, 0], self.zs[1].at[0])
 
         def one(i):
             x, y = i // NY, rem(i, NY)
@@ -497,25 +533,25 @@
         at = self.at
         over_x, over_y = self.early_p2()
         to_x, to_y = self.early_p1()
-        head, tail = pl.ds(0, CUT), pl.ds(CUT, ROWS - CUT)
+        head, tail = cut(CUTS_S[0])
         over_x.wait_recv()
-        total = self.s[0, at.z, at.x, at.c, at.oy, head].astype(F32) + self.erd0[...].astype(F32)
+        total = self.s[0, at.z, at.x, at.c, at.oy, head].astype(F32) + self.erd[head].astype(F32)
         self.s[0, at.z, at.x, at.c, at.oy, head] = total.astype(BF)
         to_y.start()
         over_y.wait_recv()
-        total = self.s[0, at.z, at.ox, at.c, at.y, tail].astype(F32) + self.erd1[...].astype(F32)
+        total = self.s[0, at.z, at.ox, at.c, at.y, tail].astype(F32) + self.erd[tail].astype(F32)
         self.s[0, at.z, at.ox, at.c, at.y, tail] = total.astype(BF)
         to_x.start()
 
     def early_finish(self):
         at = self.at
-        for copy in self.early_p1():
-            copy.wait_recv()
+        self.got(self.s.at[0, 0:1, :, 0, 0], self.p1[1].at[0])
         total = self.s[0, at.z, at.x, at.c, at.y].astype(F32) + self.erx[...].astype(F32)
         return total + self.ery[...].astype(F32)
 
     def early_drain(self):
-        self.c_copy(0).wait_send()
+        for k in range(NZ):
+            self.early_copy(k).wait_send()
         self.sent(self.s.at[0, 0:1, 0, 0, 0], self.p2[0].at[0])
         self.sent(self.s.at[0, 0:1, :, 0, 0], self.p1[0].at[0])
         self.sent(self.s.at[0, 0:3, :, 0], self.zs[0].at[0])
@@ -671,15 +707,15 @@
     q, k, v, o, inner, outer, qb, vb, ob, g1, s1, ub, g2, s2, inner_bias, pad, hidden, grad, lengths,
     out, igrad, dq, dk, dv, do, di, du, dsmall, saved,
     g, gv, wd, u, page, cot, dead, mask, small, hid, qkv, outp, xt, hidt, ctxt, actt,
-    n1, inv1, acc1, acc2, dst, bias, vec, ib, vg, ibg,
-    sv, r1, rd0, rd1, rx, ry, rz, early, erd0, erd1, erx, ery, vc, vx, vy, vz,
+    n1, acc1, acc2, bias, vec, ib, vg, ibg,
+    sv, r1, rd, rx, ry, rz, early, erd, erx, ery, vc, vx, vy, vz,
     zs, zr, p1s, p1r, p2s, p2r, cs, cr, vs, vr, es, er,
     csr, q2r, q1r, zsr, wr, loads, saves, stores,
 ):
     at = Place(stride)
     gather = Gather(at, g, (zs, zr), (p1s, p1r), (p2s, p2r), (cs, cr))
     scatter = Scatter(
-        at, g, r1, rd0, rd1, rx, ry, rz, early, (erd0, erd1, erx, ery), gather.sent, (cs, csr), (p2s, q2r), (p1s, q1r), (zs, zsr)
+        at, g, r1, rd, rx, ry, rz, early, (erd, erx, ery), gather.sent, gather.got, (cs, csr), (p2s, q2r), (p1s, q1r), (zs, zsr)
     )
     vector = VectorScatter(at, sv, vc, vx, vy, vz, (vs, wr))
 
@@ -785,7 +821,7 @@
 
     def save(pair):
         cols = tile(pair, 1024)
-        return pltpu.make_async_copy(u.at[:, cols], saved.at[:, cols], saves.at[pair])
+        return pltpu.make_async_copy(u.at[:, cols], saved.at[:, cols], saves.at[0])
 
     def attend(pair):
         at_q, at_k, at_v = tile(pair, 128), tile(pair + 6, 128), tile(pair + 12, 128)
@@ -818,7 +854,7 @@
         inverse = lax.rsqrt(mean(center * center) + EPSILON)
         normed = center * inverse
         n1[rows, :] = normed
-        inv1[rows, :] = jnp.broadcast_to(inverse, (64, 128))
+        bias[rows, 64:128] = jnp.broadcast_to(inverse, (64, 64))
         hid[rows, :] = (normed * vec[G1 : G1 + 1] + vec[S1 : S1 + 1]).astype(BF)
 
     def turn_hidden(i):
@@ -828,7 +864,7 @@
         loop(3, attended)
         loop(8, first_norm)
         loop(3, turn_hidden)
-        loop(6, lambda i: save(i).wait())
+        pltpu.make_async_copy(u, saved, saves.at[0]).wait()
 
     def feed(i):
         cols = tile(i, 384)
@@ -844,7 +880,7 @@
             u[rows, pl.ds(pl.multiple_of(3072 + 384 * i, 384), 384)] = (cdf + value * density).astype(BF)
 
         loop(8, one)
-        actt[cols, :] = u[:, cols].T
+        actt[i // NX, rem(i, NX)] = u[:, cols].T.reshape(NC, NY, ROWS, 512)
 
     def outer_left():
         acc1[:, 0:COLS] = product(u[:, 0:3072], g[4].reshape(8 * COLS, COLS))
@@ -861,7 +897,7 @@
             rows = tile(i, 64)
             dy = cot[rows, :].astype(F32)
             vg[S2 : S2 + 1] += column(dy)
-            bias[rows, :] = jnp.broadcast_to(mean(dy * vec[G2 : G2 + 1]), (64, 128))
+            bias[rows, 0:64] = jnp.broadcast_to(mean(dy * vec[G2 : G2 + 1]), (64, 64))
 
         loop(8, one)
 
@@ -933,17 +969,21 @@
         out_over.start()
         keep.start()
 
-    def outer_grad(half, slot):
-        def one(i):
-            cols = slice(COLS * half, COLS * half + COLS)
-            value = product(actt[tile(i, 1536), :], low[:, cols]).astype(BF)
-            g[slot, pl.ds(2 * i, 2)] = value.reshape(2, NX, NC, NY, ROWS, COLS)
-
-        loop(2, one)
+    def outer_first(step):
+        x, y = ((at.ox, at.oy), (at.ox, at.y), (at.x, at.oy), (at.x, at.y))[step]
+        value = product(actt[:, x, :, y].reshape(2 * COLS, 512), low[:, 0:COLS]).astype(BF)
+        g[1, :, x, :, y] = value.reshape(NZ, NC, ROWS, COLS)
+
+    def outer_second(k):
+        z = at.above(k)
+        value = product(actt[z].reshape(2 * COLS, 512), low[:, COLS:]).astype(BF)
+        g[0, z] = value.reshape(NX, NC, NY, ROWS, COLS)
 
     def load(part):
         cols = pl.ds(3072 * part, 3072)
         return pltpu.make_async_copy(saved.at[:, cols], u.at[:, cols], loads.at[1])
+
+    load(0).start()
 
     def inner_back(i):
         weight = [g[4 + half, i].reshape(2 * COLS, COLS) for half in range(2)]
@@ -980,7 +1020,7 @@
         vg[G1 : G1 + 1] += column(up * normed)
         vg[S1 : S1 + 1] += column(up)
         scaled = up * vec[G1 : G1 + 1]
-        inverse = inv1[rows, 0:1]
+        inverse = bias[rows, 64:65]
         back = inverse * (scaled - mean(scaled) - normed * mean(scaled * normed))
         acc2[rows, :] = back
         short = back.astype(BF)
@@ -990,6 +1030,8 @@
     def context_back(i):
         cols = tile(i, 256)
         hid[:, cols] = product_right(low[...], wd[cols, 3 * WIDTH : 4 * WIDTH]).astype(BF)
+
+    dst = hidt.at[pl.ds(0, 512), :]
 
     def attend_back(pair):
         at_q, at_k, at_v = tile(pair, 128), tile(pair + 6, 128), tile(pair + 12, 128)
@@ -1037,7 +1079,7 @@
             rows, cols = pl.ds(ROWS + 24 * (index - 2), 24), pl.ds(0, WIDTH)
             target = di.at[:, pl.ds(WIDTH * (index - 2), WIDTH)] if index < 6 else (dv, do, dq, dk)[index - 6]
         place = acc1.at[rows, cols]
-        return place, pltpu.make_async_copy(place, target, stores.at[index])
+        return place, pltpu.make_async_copy(place, target, stores.at[0])
 
     def store(index, value):
         place, copy = result(index)
@@ -1059,10 +1101,6 @@
         load(1).start()
         loop(3, context_back)
         load(1).wait()
-
-    def outer_second():
-        outer_grad(1, 0)
-        load(0).start()
 
     def output_grad():
         weight_grad(4, 1, ctxt, low[...])
@@ -1079,6 +1117,7 @@
             "diagonal": scatter.diagonal,
             "plane": scatter.plane,
             "finish": finish,
+            "early_start": scatter.early_start,
             "early_core": scatter.early_core,
             "early_plane": scatter.early_plane,
             "early_diagonal": scatter.early_diagonal,
@@ -1089,7 +1128,10 @@
             "vector_finish": vector_finish,
             "out": out_start,
             "grad": grad_start,
-            "outer_first": lambda: outer_grad(0, 1),
+            "start_first": scatter.start_first,
+            "core_first": scatter.core_first,
+            "core_rest": scatter.core_rest,
+            "outer_first": outer_first,
             "outer_second": outer_second,
             "inner_grad": inner_grad,
             "first_back": first_grad,
@@ -1110,8 +1152,8 @@
     )
     keep.wait()
     keep_in.wait()
-    for index in range(10):
-        result(index)[1].wait()
+    stored = acc1.at[pl.ds(0, 3 * ROWS)]
+    pltpu.make_async_copy(stored, stored, stores.at[0]).wait()
     out_over.wait_recv()
     grad_over.wait_recv()
     for n in range(1, CHUNKS):
@@ -1163,47 +1205,43 @@
             low(WIDTH, 512),
             low(WIDTH, 512),
             low(WIDTH, 512),
-            low(4 * WIDTH, 512),
-            full(512, WIDTH),
-            full(512, 128),
+            low(NZ, NX, NC, NY, ROWS, 512),
             full(512, WIDTH),
             full(512, WIDTH),
-            low(512, 512),
+            full(512, WIDTH),
             full(512, 128),
             full(8, WIDTH),
             full(8, 4 * WIDTH),
             full(8, WIDTH),
             full(8, 4 * WIDTH),
             full(NZ, NX, NC, NY, 16, 128),
-            low(CHUNKS, NZ, NX, NY, ROWS, COLS),
-            low(CHUNKS - 1, NZ, CUT, COLS),
-            low(CHUNKS - 1, NZ, ROWS - CUT, COLS),
+            low(CHUNKS - 1, NZ, NX, NY, ROWS, COLS),
+            low(CHUNKS - 1, NZ, ROWS, COLS),
             low(CHUNKS - 1, NZ, ROWS, COLS),
             low(CHUNKS - 1, NZ, ROWS, COLS),
             low(CHUNKS - 1, NZ - 1, ROWS, COLS),
             low(NZ - 1, NX, NY, ROWS, COLS),
-            low(CUT, COLS),
-            low(ROWS - CUT, COLS),
+            low(ROWS, COLS),
             low(ROWS, COLS),
             low(ROWS, COLS),
             full(NZ, NX, NY, 16, 128),
             full(NZ, NY, 16, 128),
             full(NZ, 16, 128),
             full(NZ - 1, 16, 128),
-            dma((CHUNKS,)), dma((CHUNKS, NZ - 1)),
+            dma((CHUNKS,)), dma((G_ALONG,)),
             dma((CHUNKS,)), dma((G_STEPS, 2)),
-            dma((CHUNKS,)), dma((G_STEPS, 2)),
-            *pair(LATE + NZ),
+            *pair(CHUNKS),
+            dma((CHUNKS + NZ + 1,)), dma((LATE + NZ,)),
             *pair(6),
             *pair(5),
-            dma((CHUNKS + 2,)),
+            dma((CHUNKS + NZ + 1,)),
             dma((S_STEPS, 2)),
-            dma((S_STEPS, 2)),
-            dma((CHUNKS, NZ - 1)),
+            dma((S_STEPS,)),
+            dma((CHUNKS,)),
             dma((6,)),
             dma((2,)),
-            dma((6,)),
-            dma((10,)),
+            dma((1,)),
+            dma((1,)),
         ],
         compiler_params=pltpu.CompilerParams(
             collective_id=0, has_side_effects=True, vmem_limit_bytes=VMEM_LIMIT

time: 157 us -> 155 us (0.987)
  Pallas kernels: 156 us -> 154 us
    pallas_call x1, Pallas kernels: 152 us -> 150 us  [layer_call(): pl.pallas_call(partial(layer_kernel, stride), out_shape=tuple(tokens + gr...]
where the time goes in v3:
time: 155 us; the launch traced here: 154 us
  Pallas kernels  154 us (99%)
    pallas_call x1, Pallas kernels, layer_call(): pl.pallas_call(partial(layer_kernel, stride), out_shape=tuple(tokens + gr...  150 us
    pallas_call x1, Pallas kernels, hand_out(): pl.pallas_call(hand_out_kernel, out_shape=tuple([jax.ShapeDtypeStruct(v.s...  3.96 us

profile of v3, /device:TPU:0, one launch (start us, length us, event | category | flops | bytes accessed | tf_op | source)
XLA Modules:
  0.0 154.4 jit_solution(1942751803443938999)
XLA Ops:
  0.7 149.6 %layer.1 = (bf16[2,256,768]{2,1,0:T(8,128)(2,1)}, bf16[2,256,768]{2,1,0:T(8,128)(2,1)}, f32[24,768]{1,0:T(8,128)}, f32[24,768]{1,0:T(8,128)}, f32[24,768]{1,0:T(...) custom-call(bf16[24,768]{1,0:T(8,128)(2,1)} %q.1, ...), custom_call_target="tpu_custom_call" | custom-call | tf_op jit(solution)/shard_map/layer/pallas_call | solution.py:1187
  150.3 4.0 %hand_out.1 = (bf16[2,256,768]{2,1,0:T(8,128)(2,1)}, bf16[2,256,768]{2,1,0:T(8,128)(2,1)}, f32[24,768]{1,0:T(8,128)}, f32[24,768]{1,0:T(8,128)}, f32[24,768]{1,0...) custom-call(bf16[2,256,768]{2,1,0:T(8,128)(2,1)} %get-tuple-element., ...), custom_call_target="tpu_custom_call" | custom-call | tf_op jit(solution)/shard_map/hand_out/pallas_call | solution.py:1273

commit v4 on v3

--- a/solution.py
+++ b/solution.py
@@ -21,7 +21,7 @@
 G_ALONG = len(COARSE) + (NZ - 1) * (len(FINE_G) + 1)
 WIDTH = 768
 CUTS_G = (64, 80, 48, 48, 64, 80)
-CUTS_S = (32, 48, 32, 48, 48, 80)
+CUTS_S = (32, 80, 64, 48, 48, 64)
 FINE = (4, 5)
 S_STEPS = FINE[0] + NZ * len(FINE)
 BF, F32 = jnp.bfloat16, jnp.float32
@@ -41,20 +41,20 @@
     "outer_right 3",
 )
 BACKWARD = (
-    "out", "outer_second 2", "outer_second 1", "outer_first 0", "early_start 2", "start_first 0",
-    "outer_first 1", "inner_back 0", "outer_second 3", "early_start 1", "outer_first 2", "outer_first 3",
-    "early_core 2", "core_first", "start_first 2", "inner_back 1", "start_first 1", "outer_second 0",
-    "inner_back 2", "inner_back 3", "core_rest", "early_start 3", "inner_grad 0", "early_start 0",
-    "early_core 1", "diagonal 1", "inner_grad 1", "early_core 0", "early_core 3", "start 2", "inner_grad 2",
-    "inner_grad 3", "hidden_back 0", "start 3", "core 2", "hidden_back 1", "hidden_back 2", "first_back",
-    "core 3", "diagonal 2", "context_back", "attend_back 0", "attend_back 1", "attend_back 2", "plane 1",
-    "output_grad", "early_plane", "diagonal 3", "attend_back 3", "attend_back 4", "attend_back 5", "value_grad",
-    "start 4", "early_diagonal", "key_grad", "query_grad", "sums", "plane 3", "start 5", "core 4",
-    "gather_vectors", "diagonal 4 1", "vector", "plane 2", "finish 1", "diagonal 4 2", "core 5", "input_back 0",
-    "diagonal 4 3", "plane 4 2", "vector_core", "input_back 1", "plane 4 1", "diagonal 5 1", "diagonal 5 2",
-    "diagonal 5 3", "diagonal 4 0", "finish 3", "diagonal 5 0", "input_back 2", "plane 4 3", "finish 0",
-    "vector_x", "grad", "plane 5 1", "plane 5 2", "finish 2", "plane 5 3", "plane 5 0", "vector_y", "plane 4 0",
-    "finish 4", "finish 5", "vector_finish",
+    "out", "outer_second 3", "outer_second 1", "outer_first 0", "start_first 0", "outer_first 1",
+    "outer_first 2", "outer_second 2", "early_start 2", "inner_back 0", "core_first", "early_start 1",
+    "early_core 2", "start_first 1", "outer_first 3", "start_first 2", "outer_second 0", "early_start 0",
+    "inner_back 1", "inner_back 2", "inner_back 3", "early_start 3", "core_rest", "inner_grad 0", "diagonal 1",
+    "early_core 3", "inner_grad 1", "early_core 1", "inner_grad 2", "early_core 0", "start 2", "inner_grad 3",
+    "hidden_back 0", "hidden_back 1", "start 3", "core 2", "hidden_back 2", "first_back", "core 3",
+    "context_back", "diagonal 2", "attend_back 0", "attend_back 1", "attend_back 2", "output_grad", "plane 1",
+    "early_plane", "diagonal 3", "attend_back 3", "attend_back 4", "attend_back 5", "early_diagonal",
+    "value_grad", "start 4", "key_grad", "sums", "query_grad", "plane 3", "start 5", "core 4", "gather_vectors",
+    "diagonal 4 1", "diagonal 4 2", "finish 1", "plane 2", "vector", "input_back 0", "core 5", "plane 4 2",
+    "finish 0", "diagonal 4 3", "vector_core", "plane 4 1", "diagonal 5 1", "input_back 1", "input_back 2",
+    "diagonal 4 0", "finish 3", "diagonal 5 2", "diagonal 5 3", "vector_x", "plane 4 3", "diagonal 5 0",
+    "plane 5 1", "grad", "plane 4 0", "plane 5 2", "plane 5 3", "finish 4", "plane 5 0", "vector_y", "finish 2",
+    "vector_finish", "finish 5",
 )
 
 

time: 155 us -> 154 us (level)
  Pallas kernels: 154 us -> 152 us
where the time goes in v4:
time: 154 us; the launch traced here: 153 us
  Pallas kernels  152 us (99%)
    pallas_call x1, Pallas kernels, layer_call(): pl.pallas_call(partial(layer_kernel, stride), out_shape=tuple(tokens + gr...  149 us
    pallas_call x1, Pallas kernels, hand_out(): pl.pallas_call(hand_out_kernel, out_shape=tuple([jax.ShapeDtypeStruct(v.s...  3.96 us

profile of v4, /device:TPU:0, one launch (start us, length us, event | category | flops | bytes accessed | tf_op | source)
XLA Modules:
  0.0 153.3 jit_solution(3793702673845845987)
XLA Ops:
  0.7 148.5 %layer.1 = (bf16[2,256,768]{2,1,0:T(8,128)(2,1)}, bf16[2,256,768]{2,1,0:T(8,128)(2,1)}, f32[24,768]{1,0:T(8,128)}, f32[24,768]{1,0:T(8,128)}, f32[24,768]{1,0:T(...) custom-call(bf16[24,768]{1,0:T(8,128)(2,1)} %q.1, ...), custom_call_target="tpu_custom_call" | custom-call | tf_op jit(solution)/shard_map/layer/pallas_call | solution.py:1187
  149.2 4.0 %hand_out.1 = (bf16[2,256,768]{2,1,0:T(8,128)(2,1)}, bf16[2,256,768]{2,1,0:T(8,128)(2,1)}, f32[24,768]{1,0:T(8,128)}, f32[24,768]{1,0:T(8,128)}, f32[24,768]{1,0...) custom-call(bf16[2,256,768]{2,1,0:T(8,128)(2,1)} %get-tuple-element., ...), custom_call_target="tpu_custom_call" | custom-call | tf_op jit(solution)/shard_map/hand_out/pallas_call | solution.py:1273
